TPU v7x, 32 devices: a whole 2x2x4 slice. The times are simulated.
32 devices in a mesh: seq: 8 (over y, x, core), tp: 4 (over z).
Axes of the slice: x: 2, y: 2, z: 4, core: 2. Of those that a mesh axis runs over, the one named last changes fastest.
Arguments:
- tokens: bfloat16 [12288, 1536], P(('seq', 'tp')), may hold values from -6 to 6
- cond_embed: bfloat16 [24, 1024], P('seq'), may hold values from -6 to 6
- caption: bfloat16 [6144, 4096], P(('seq', 'tp')), may hold values from -6 to 6
- clip_len: int32 [8, 3], P('seq'), may hold values from 1 to 1024, 1536 in all within a row
- rope_off: int32 [8, 3], P('seq'), may hold values from 0 to 2047
- text_len: int32 [8, 3], P('seq'), may hold values from 32 to 256
- query_proj: bfloat16 [1536, 1536], P(None, 'tp'), may hold values from -0.15625 to 0.15625
- key_proj: bfloat16 [1536, 1536], P(None, 'tp'), may hold values from -0.15625 to 0.15625
- value_proj: bfloat16 [1536, 1536], P(None, 'tp'), may hold values from -0.15625 to 0.15625
- out_proj: bfloat16 [1536, 1536], P('tp'), may hold values from -1.5 to 1.5
- gate_proj: bfloat16 [1536, 4096], P(None, 'tp'), may hold values from -0.15625 to 0.15625
- up_proj: bfloat16 [1536, 4096], P(None, 'tp'), may hold values from -0.15625 to 0.15625
- down_proj: bfloat16 [4096, 1536], P('tp'), may hold values from -0.09375 to 0.09375
- key_text: bfloat16 [4096, 1536], P(None, 'tp'), may hold values from -0.09375 to 0.09375
- value_text: bfloat16 [4096, 1536], P(None, 'tp'), may hold values from -0.09375 to 0.09375
- ada_weight: bfloat16 [1024, 6, 1536], P(None, None, 'tp'), may hold values from -0.1875 to 0.1875
- ada_bias: bfloat16 [6, 1536], P(None, 'tp'), may hold values from -1.5 to 1.5
- query_gain: bfloat16 [24, 64], P('tp'), may hold values from 0.25 to 1.75
- key_gain: bfloat16 [24, 64], P('tp'), may hold values from 0.25 to 1.75
- text_gain: bfloat16 [24, 64], P('tp'), may hold values from 0.25 to 1.75
- text_gate: bfloat16 [24], P('tp'), may hold values from 0.29882812 to 1.1953125
- cotangent: bfloat16 [12288, 1536], P(('seq', 'tp')), may hold values from -6 to 6
Outputs:
- output: bfloat16 [12288, 1536], P(('seq', 'tp'))
- grad_tokens: bfloat16 [12288, 1536], P(('seq', 'tp'))
- grad_query_proj: float32 [1536, 1536], P('seq', 'tp')
- grad_key_proj: float32 [1536, 1536], P('seq', 'tp')
- grad_value_proj: float32 [1536, 1536], P('seq', 'tp')
- grad_out_proj: float32 [1536, 1536], P('tp', 'seq')
- grad_gate_proj: float32 [1536, 4096], P('seq', 'tp')
- grad_up_proj: float32 [1536, 4096], P('seq', 'tp')
- grad_down_proj: float32 [4096, 1536], P('tp', 'seq')
- grad_key_text: float32 [4096, 1536], P('seq', 'tp')
- grad_value_text: float32 [4096, 1536], P('seq', 'tp')
- grad_ada_weight: float32 [1024, 6, 1536], P('seq', None, 'tp')
- grad_ada_bias: float32 [6, 1536], P(None, 'tp')
- grad_query_gain: float32 [24, 64], P('tp')
- grad_key_gain: float32 [24, 64], P('tp')
- grad_text_gain: float32 [24, 64], P('tp')
- grad_text_gate: float32 [24], P('tp')
All inputs are finite; a program needn't handle non-finite values.
Results may differ from a plain program's by a relative error of at most 0.014.
Values may be sent and summed in bfloat16 or wider, within the bound.
A program may use at most 256 MiB of HBM per device.

v0:
```python
import jax
import jax.numpy as jnp
from jax import lax
from jax.sharding import PartitionSpec as P

epsilon = 1e-06
highest = lax.Precision.HIGHEST


def rms_parts(values):
    factor = lax.rsqrt(jnp.mean(values * values, axis=-1, keepdims=True) + epsilon)
    return (values * factor, factor)


def rms_back(grad, normed, factor):
    return factor * (grad - normed * jnp.mean(grad * normed, axis=-1, keepdims=True))


def rotate(values, cosine, sine):
    half = values.shape[-1] // 2
    first = values[..., :half]
    second = values[..., half:]
    return jnp.concatenate(
        [first * cosine - second * sine, first * sine + second * cosine], axis=-1
    )


def unrotate(grads, cosine, sine):
    half = grads.shape[-1] // 2
    first = grads[..., :half]
    second = grads[..., half:]
    return jnp.concatenate(
        [first * cosine + second * sine, second * cosine - first * sine], axis=-1
    )


def row_block(values, start, count):
    return lax.dynamic_slice_in_dim(values, start, count, 0)


def body(
    tokens,
    cond_embed,
    caption,
    clip_len,
    rope_off,
    text_len,
    query_proj,
    key_proj,
    value_proj,
    out_proj,
    gate_proj,
    up_proj,
    down_proj,
    key_text,
    value_text,
    ada_weight,
    ada_bias,
    query_gain,
    key_gain,
    text_gain,
    text_gate,
    cotangent,
):
    bf_type = jnp.bfloat16
    f_type = jnp.float32
    n_ranks = lax.axis_size("tp")
    local_rows = tokens.shape[0]
    first_row = lax.axis_index("tp") * local_rows
    group = local_rows * n_ranks
    clips = cond_embed.shape[0]
    heads_here = query_gain.shape[0]
    head_dim = query_gain.shape[1]
    inner = heads_here * head_dim
    scale = head_dim ** (-0.5)
    block = 512
    n_blocks = group // block
    lengths = clip_len[0]
    starts = jnp.cumsum(lengths) - lengths
    row_index = jnp.arange(group, dtype=jnp.int32)
    member = (row_index[:, None] >= starts[None, :]) & (
        row_index[:, None] < (starts + lengths)[None, :]
    )
    member_int = member.astype(jnp.int32)
    member_all = member.astype(f_type)
    member_own = row_block(member_all, first_row, local_rows)
    clip_of = jnp.sum(member_int * jnp.arange(clips, dtype=jnp.int32)[None, :], axis=1)
    position = jnp.sum(
        member_int * (row_index[:, None] - starts[None, :] + rope_off[0][None, :]), axis=1
    ).astype(f_type)
    half = head_dim // 2
    inverse = 10000.0 ** (-jnp.arange(half, dtype=f_type) / half)
    angle = position[:, None] * inverse[None, :]
    cosine = jnp.cos(angle)[:, None, :]
    sine = jnp.sin(angle)[:, None, :]
    text_total = caption.shape[0] * n_ranks
    per_clip = text_total // clips
    text_index = jnp.arange(text_total, dtype=jnp.int32)
    text_clip = text_index // per_clip
    text_member = (text_clip[:, None] == jnp.arange(clips, dtype=jnp.int32)[None, :]).astype(
        jnp.int32
    )
    text_limit = jnp.sum(text_member * text_len[0][None, :], axis=1)
    text_valid = text_index - text_clip * per_clip < text_limit
    silu_cond = jax.nn.silu(cond_embed.astype(f_type)).astype(bf_type)
    mod_local = (
        jnp.einsum("ck,kjd->cjd", silu_cond, ada_weight, preferred_element_type=f_type)
        + ada_bias.astype(f_type)[None]
    )
    modulation = lax.all_gather(mod_local, "tp", axis=2, tiled=True)

    def token_mod(which, weights):
        return jnp.dot(weights, modulation[:, which, :], precision=highest)

    shift_attn = token_mod(0, member_own)
    scale_attn = token_mod(1, member_own)
    gate_attn = token_mod(2, member_own)
    shift_ffn = token_mod(3, member_own)
    scale_ffn = token_mod(4, member_own)
    gate_ffn = token_mod(5, member_own)
    rows_in = tokens.astype(f_type)
    normed_own, factor_own = rms_parts(rows_in)
    outgoing = (normed_own * (1.0 + scale_attn) + shift_attn).astype(bf_type)
    modin, text_all = (
        lax.all_gather(outgoing, "tp", axis=0, tiled=True),
        lax.all_gather(caption, "tp", axis=0, tiled=True),
    )
    query_pre = jnp.dot(modin, query_proj, preferred_element_type=f_type).reshape(
        group, heads_here, head_dim
    )
    key_pre = jnp.dot(modin, key_proj, preferred_element_type=f_type).reshape(
        group, heads_here, head_dim
    )
    value_low = (
        jnp.dot(modin, value_proj, preferred_element_type=f_type)
        .astype(bf_type)
        .reshape(group, heads_here, head_dim)
    )
    query_hat, query_factor = rms_parts(query_pre)
    key_hat, key_factor = rms_parts(key_pre)
    qgain = query_gain.astype(f_type)
    kgain = key_gain.astype(f_type)
    tgain = text_gain.astype(f_type)
    query_rot = rotate(query_hat * qgain, cosine, sine).astype(bf_type)
    key_rot = rotate(key_hat * kgain, cosine, sine).astype(bf_type)
    tkey_pre = jnp.dot(text_all, key_text, preferred_element_type=f_type).reshape(
        text_total, heads_here, head_dim
    )
    tkey_hat, tkey_factor = rms_parts(tkey_pre)
    text_keys = (tkey_hat * tgain).astype(bf_type)
    text_values = (
        jnp.dot(text_all, value_text, preferred_element_type=f_type)
        .astype(bf_type)
        .reshape(text_total, heads_here, head_dim)
    )

    def self_scores(query_block, clip_block):
        scores = (
            jnp.einsum("qhd,khd->hqk", query_block, key_rot, preferred_element_type=f_type) * scale
        )
        return jnp.where((clip_block[:, None] == clip_of[None, :])[None], scores, -1e30)

    def cross_scores(query_block, clip_block):
        scores = (
            jnp.einsum("qhd,khd->hqk", query_block, text_keys, preferred_element_type=f_type)
            * scale
        )
        allowed = (clip_block[:, None] == text_clip[None, :]) & text_valid[None, :]
        return jnp.where(allowed[None], scores, -1e30)

    def forward_block(start):
        query_block = row_block(query_rot, start, block)
        clip_block = row_block(clip_of, start, block)
        scores = self_scores(query_block, clip_block)
        top = jnp.max(scores, axis=-1, keepdims=True)
        expo = jnp.exp(scores - top)
        total = jnp.sum(expo, axis=-1, keepdims=True)
        self_block = jnp.einsum(
            "hqk,khd->qhd", (expo / total).astype(bf_type), value_low, preferred_element_type=f_type
        )
        cscores = cross_scores(query_block, clip_block)
        ctop = jnp.max(cscores, axis=-1, keepdims=True)
        cexpo = jnp.exp(cscores - ctop)
        ctotal = jnp.sum(cexpo, axis=-1, keepdims=True)
        cross_block = jnp.einsum(
            "hqk,khd->qhd",
            (cexpo / ctotal).astype(bf_type),
            text_values,
            preferred_element_type=f_type,
        )
        return (self_block, cross_block, top, total, ctop, ctotal)

    block_starts = jnp.arange(n_blocks, dtype=jnp.int32) * block
    self_out, cross_out, top_self, total_self, top_cross, total_cross = lax.map(
        forward_block, block_starts
    )
    self_out = self_out.reshape(group, heads_here, head_dim)
    cross_out = cross_out.reshape(group, heads_here, head_dim)
    tgate = jnp.tanh(text_gate.astype(f_type))[:, None]
    mixed = (self_out + tgate * cross_out).astype(bf_type).reshape(group, inner)
    attn_own = lax.psum_scatter(
        jnp.dot(
            row_block(mixed, jnp.int32(0), local_rows * lax.axis_size("tp")),
            out_proj,
            preferred_element_type=f_type,
        ),
        "tp",
        scatter_dimension=0,
        tiled=True,
    )
    hidden_own = rows_in + gate_attn * attn_own
    normed_mid, factor_mid = rms_parts(hidden_own)
    ffn_in = lax.all_gather(
        (normed_mid * (1.0 + scale_ffn) + shift_ffn).astype(bf_type), "tp", axis=0, tiled=True
    )
    gate_pre = jnp.dot(ffn_in, gate_proj, preferred_element_type=f_type)
    up_pre = jnp.dot(ffn_in, up_proj, preferred_element_type=f_type)
    gate_silu = jax.nn.silu(gate_pre)
    act = (gate_silu * up_pre).astype(bf_type)
    ffn_own = lax.psum_scatter(
        jnp.dot(
            row_block(act, jnp.int32(0), lax.axis_size("tp") * local_rows),
            down_proj,
            preferred_element_type=f_type,
        ).astype(jnp.bfloat16),
        "tp",
        scatter_dimension=0,
        tiled=True,
    ).astype(jnp.float32)
    output = (hidden_own + gate_ffn * ffn_own).astype(bf_type)
    grad_y = cotangent.astype(f_type)
    grad_ffn_all = lax.all_gather((gate_ffn * grad_y).astype(bf_type), "tp", axis=0, tiled=True)
    grad_act = jnp.dot(grad_ffn_all, down_proj.T, preferred_element_type=f_type)
    gate_sig = jax.nn.sigmoid(gate_pre)
    grad_up = (grad_act * gate_silu).astype(bf_type)
    grad_gate = (grad_act * up_pre * gate_sig * (1.0 + gate_pre * (1.0 - gate_sig))).astype(bf_type)
    d_down = jnp.einsum("tf,td->fd", act, grad_ffn_all, preferred_element_type=f_type)
    d_gate = jnp.einsum("td,tf->df", ffn_in, grad_gate, preferred_element_type=f_type)
    d_up = jnp.einsum("td,tf->df", ffn_in, grad_up, preferred_element_type=f_type)
    start = jnp.int32(0)
    grad_mid = lax.psum_scatter(
        jnp.dot(
            row_block(grad_gate, start, local_rows * lax.axis_size("tp")),
            gate_proj.T,
            preferred_element_type=f_type,
        )
        + jnp.dot(
            row_block(grad_up, start, local_rows * lax.axis_size("tp")),
            up_proj.T,
            preferred_element_type=f_type,
        ),
        "tp",
        scatter_dimension=0,
        tiled=True,
    )
    grad_hidden = grad_y + rms_back(grad_mid * (1.0 + scale_ffn), normed_mid, factor_mid)
    grad_attn_own = (gate_attn * grad_hidden).astype(bf_type)
    grad_attn_all = lax.all_gather(grad_attn_own, "tp", axis=0, tiled=True)
    d_outproj = jnp.einsum("tk,td->kd", mixed, grad_attn_all, preferred_element_type=f_type)
    grad_mixed = jnp.dot(grad_attn_all, out_proj.T, preferred_element_type=f_type).reshape(
        group, heads_here, head_dim
    )
    grad_self = grad_mixed.astype(bf_type)
    grad_cross = (tgate * grad_mixed).astype(bf_type)
    d_tgate = jnp.sum(grad_mixed * cross_out, axis=(0, 2)) * (1.0 - tgate[:, 0] * tgate[:, 0])

    def backward_block(carry, pieces):
        acc_key, acc_value, acc_tkey, acc_tvalue = carry
        start, top, total, ctop, ctotal = pieces
        query_block = row_block(query_rot, start, block)
        clip_block = row_block(clip_of, start, block)
        gself_block = row_block(grad_self, start, block)
        gcross_block = row_block(grad_cross, start, block)
        probs = jnp.exp(self_scores(query_block, clip_block) - top) / total
        grad_probs = jnp.einsum(
            "qhd,khd->hqk", gself_block, value_low, preferred_element_type=f_type
        )
        grad_scores = (
            probs * (grad_probs - jnp.sum(grad_probs * probs, axis=-1, keepdims=True))
        ).astype(bf_type)
        grad_query = jnp.einsum("hqk,khd->qhd", grad_scores, key_rot, preferred_element_type=f_type)
        acc_key = acc_key + jnp.einsum(
            "hqk,qhd->khd", grad_scores, query_block, preferred_element_type=f_type
        )
        acc_value = acc_value + jnp.einsum(
            "hqk,qhd->khd", probs.astype(bf_type), gself_block, preferred_element_type=f_type
        )
        cprobs = jnp.exp(cross_scores(query_block, clip_block) - ctop) / ctotal
        grad_cprobs = jnp.einsum(
            "qhd,khd->hqk", gcross_block, text_values, preferred_element_type=f_type
        )
        grad_cscores = (
            cprobs * (grad_cprobs - jnp.sum(grad_cprobs * cprobs, axis=-1, keepdims=True))
        ).astype(bf_type)
        grad_query = grad_query + jnp.einsum(
            "hqk,khd->qhd", grad_cscores, text_keys, preferred_element_type=f_type
        )
        acc_tkey = acc_tkey + jnp.einsum(
            "hqk,qhd->khd", grad_cscores, query_block, preferred_element_type=f_type
        )
        acc_tvalue = acc_tvalue + jnp.einsum(
            "hqk,qhd->khd", cprobs.astype(bf_type), gcross_block, preferred_element_type=f_type
        )
        return ((acc_key, acc_value, acc_tkey, acc_tvalue), grad_query)

    zero_rows = jnp.zeros((group, heads_here, head_dim), f_type)
    zero_text = jnp.zeros((text_total, heads_here, head_dim), f_type)
    (acc_key, acc_value, acc_tkey, acc_tvalue), grad_qblocks = lax.scan(
        backward_block,
        (zero_rows, zero_rows, zero_text, zero_text),
        (block_starts, top_self, total_self, top_cross, total_cross),
    )
    grad_qn = unrotate(grad_qblocks.reshape(group, heads_here, head_dim) * scale, cosine, sine)
    d_qgain = jnp.sum(grad_qn * query_hat, axis=0)
    grad_query = (
        rms_back(grad_qn * qgain, query_hat, query_factor).astype(bf_type).reshape(group, inner)
    )
    grad_kn = unrotate(acc_key * scale, cosine, sine)
    d_kgain = jnp.sum(grad_kn * key_hat, axis=0)
    grad_key = rms_back(grad_kn * kgain, key_hat, key_factor).astype(bf_type).reshape(group, inner)
    grad_value = acc_value.astype(bf_type).reshape(group, inner)
    grad_tkn = acc_tkey * scale
    d_tgain = jnp.sum(grad_tkn * tkey_hat, axis=0)
    grad_tkey = (
        rms_back(grad_tkn * tgain, tkey_hat, tkey_factor).astype(bf_type).reshape(text_total, inner)
    )
    grad_tvalue = acc_tvalue.astype(bf_type).reshape(text_total, inner)
    d_query = jnp.einsum("td,tk->dk", modin, grad_query, preferred_element_type=f_type)
    d_key = jnp.einsum("td,tk->dk", modin, grad_key, preferred_element_type=f_type)
    d_value = jnp.einsum("td,tk->dk", modin, grad_value, preferred_element_type=f_type)
    d_keytext = jnp.einsum("td,tk->dk", text_all, grad_tkey, preferred_element_type=f_type)
    d_valtext = jnp.einsum("td,tk->dk", text_all, grad_tvalue, preferred_element_type=f_type)
    start = jnp.int32(0)
    grad_modin = lax.psum_scatter(
        jnp.dot(
            row_block(grad_query, start, local_rows * lax.axis_size("tp")),
            query_proj.T,
            preferred_element_type=f_type,
        )
        + jnp.dot(
            row_block(grad_key, start, local_rows * lax.axis_size("tp")),
            key_proj.T,
            preferred_element_type=f_type,
        )
        + jnp.dot(
            row_block(grad_value, start, local_rows * lax.axis_size("tp")),
            value_proj.T,
            preferred_element_type=f_type,
        ),
        "tp",
        scatter_dimension=0,
        tiled=True,
    )
    grad_tokens = (
        grad_hidden + rms_back(grad_modin * (1.0 + scale_attn), normed_own, factor_own)
    ).astype(bf_type)
    stacked = jnp.stack(
        [
            grad_modin,
            grad_modin * normed_own,
            grad_hidden * attn_own,
            grad_mid,
            grad_mid * normed_mid,
            grad_y * ffn_own,
        ],
        axis=0,
    )
    per_clip_grad = jnp.einsum("tc,jtd->cjd", member_own, stacked, precision=highest)
    grad_mod = lax.psum_scatter(per_clip_grad, "tp", scatter_dimension=2, tiled=True)
    d_adaw = jnp.einsum("ck,cjd->kjd", silu_cond.astype(f_type), grad_mod, precision=highest)
    d_adab = jnp.sum(grad_mod, axis=0)
    summed = (
        lax.psum_scatter(d_query, "seq", scatter_dimension=0, tiled=True),
        lax.psum_scatter(d_key, "seq", scatter_dimension=0, tiled=True),
        lax.psum_scatter(d_value, "seq", scatter_dimension=0, tiled=True),
        lax.psum_scatter(d_gate, "seq", scatter_dimension=0, tiled=True),
        lax.psum_scatter(d_up, "seq", scatter_dimension=0, tiled=True),
        lax.psum_scatter(d_keytext, "seq", scatter_dimension=0, tiled=True),
        lax.psum_scatter(d_valtext, "seq", scatter_dimension=0, tiled=True),
        lax.psum_scatter(d_adaw, "seq", scatter_dimension=0, tiled=True),
        lax.psum_scatter(d_outproj, "seq", scatter_dimension=1, tiled=True),
        lax.psum_scatter(d_down, "seq", scatter_dimension=1, tiled=True),
    )
    smalls = lax.psum((d_adab, d_qgain, d_kgain, d_tgain, d_tgate), "seq")
    return (
        output,
        grad_tokens,
        summed[0],
        summed[1],
        summed[2],
        summed[8],
        summed[3],
        summed[4],
        summed[9],
        summed[5],
        summed[6],
        summed[7],
        smalls[0],
        smalls[1],
        smalls[2],
        smalls[3],
        smalls[4],
    )


def solution(mesh):
    in_specs = (
        P(("seq", "tp"), None),
        P("seq", None),
        P(("seq", "tp"), None),
        P("seq", None),
        P("seq", None),
        P("seq", None),
        P(None, "tp"),
        P(None, "tp"),
        P(None, "tp"),
        P("tp", None),
        P(None, "tp"),
        P(None, "tp"),
        P("tp", None),
        P(None, "tp"),
        P(None, "tp"),
        P(None, None, "tp"),
        P(None, "tp"),
        P("tp", None),
        P("tp", None),
        P("tp", None),
        P("tp"),
        P(("seq", "tp"), None),
    )
    out_specs = (
        P(("seq", "tp"), None),
        P(("seq", "tp"), None),
        P("seq", "tp"),
        P("seq", "tp"),
        P("seq", "tp"),
        P("tp", "seq"),
        P("seq", "tp"),
        P("seq", "tp"),
        P("tp", "seq"),
        P("seq", "tp"),
        P("seq", "tp"),
        P("seq", None, "tp"),
        P(None, "tp"),
        P("tp", None),
        P("tp", None),
        P("tp", None),
        P("tp"),
    )
    return jax.shard_map(body, mesh=mesh, in_specs=in_specs, out_specs=out_specs, check_vma=False)
```

profile of v0, /device:TPU:0, one launch (start us, length us, event | category | flops | bytes accessed | tf_op | source)
XLA Modules:
  0.0 2309.5 jit_solution(3742469596399835635)
XLA Ops:
  14.3 15.2 all_gather.18
  39.4 86.3 %all-gather.6.cloned.1.call-done = bf16[1536,1536]{1,0:T(8,128)(2,1)} async-done(((bf16[384,1536]{1,0:T(8,128)(2,1)}), bf16[1536,1536]{1,0:T(8,128)(2,1)}) %all-gather.6.cloned.1.call-update) | async-done | bytes 4718608 | tf_op jit(solution)/shard_map/all_gather | solution.py:125
  142.2 98.8 %all-gather.8.cloned.1.call-done = bf16[768,4096]{1,0:T(8,128)(2,1)} async-done(((bf16[192,4096]{1,0:T(8,128)(2,1)}), bf16[768,4096]{1,0:T(8,128)(2,1)}) %all-gather.8.cloned.1.call-update) | async-done | bytes 6291472 | tf_op jit(solution)/shard_map/all_gather | solution.py:126
  252.3 205.9 %while.40 = (s32[]{:T(128)}, f32[3,512,6,64]{1,0,3,2:T(4,128)}, f32[3,512,6,64]{1,0,3,2:T(4,128)}, f32[3,6,512,1]{2,1,3,0:T(8,128)S(1)}, f32[3,6,512,1]{2,1,3,0:...) while((s32[]{:T(128)}, f32[3,512,6,64]{1,0,3,2:T(4,128)}, ...), condition=%wide.region_13.14_spmd.clone, body=%wide.region_8.13_spmd.clone.sunk | while | flops 1898440704 | bytes 107623464 | solution.py:194
  267.6 16.1 dynamic_update_slice.43
  294.7 7.7 fusion.233
  305.2 16.1 dynamic_update_slice.42
  336.0 16.1 dynamic_update_slice.43
  363.1 7.7 fusion.233
  373.6 16.1 dynamic_update_slice.42
  404.5 16.1 dynamic_update_slice.43
  431.5 7.7 fusion.233
  442.0 16.1 dynamic_update_slice.42
  473.5 156.2 %reduce-scatter.18.cloned.1.call-done = f32[384,1536]{1,0:T(8,128)} async-done(((f32[1536,1536]{1,0:T(8,128)}), f32[384,1536]{1,0:T(8,128)}) %reduce-scatter.18.cloned.1.call-update) | async-done | bytes 2359312 | tf_op jit(solution)/shard_map/reduce_scatter | solution.py:201
  643.2 85.9 %all-gather.10.cloned.1.call-done = bf16[1536,1536]{1,0:T(8,128)(2,1)} async-done(((bf16[384,1536]{1,0:T(8,128)(2,1)}), bf16[1536,1536]{1,0:T(8,128)(2,1)}) %all-gather.10.cloned.1.call-update) | async-done | bytes 4718608 | tf_op jit(solution)/shard_map/all_gather | solution.py:213
  729.1 10.3 fusion.117
  746.3 72.1 %all-gather.12.cloned.1.call-done = bf16[1536,1536]{1,0:T(8,128)(2,1)} async-done(((bf16[384,1536]{1,0:T(8,128)(2,1)}), bf16[1536,1536]{1,0:T(8,128)(2,1)}) %all-gather.12.cloned.1.call-update) | async-done | bytes 4718608 | tf_op jit(solution)/shard_map/all_gather | solution.py:232
  818.4 13.9 multiply_convert_fusion.2
  832.3 8.3 fusion.118
  840.6 8.4 convolution_add_fusion.3
  849.1 8.7 convolution_convert_fusion
  857.9 151.1 %reduce-scatter.22.cloned.1.call-done = f32[384,1536]{1,0:T(8,128)} async-done(((f32[1536,1536]{1,0:T(8,128)}), f32[384,1536]{1,0:T(8,128)}) %reduce-scatter.22.cloned.1.call-update) | async-done | bytes 2359312 | tf_op jit(solution)/shard_map/reduce_scatter | solution.py:241
  1013.2 84.2 %reduce-scatter.20.cloned.1.call-done = bf16[384,1536]{1,0:T(8,128)(2,1)} async-done(((bf16[1536,1536]{1,0:T(8,128)(2,1)}), bf16[384,1536]{1,0:T(8,128)(2,1)}) %reduce-scatter.20.cloned.1.call-update) | async-done | bytes 1179664 | tf_op jit(solution)/shard_map/reduce_scatter | solution.py:220
  1105.6 88.7 %all-gather.14.cloned.1.call-done = bf16[1536,1536]{1,0:T(8,128)(2,1)} async-done(((bf16[384,1536]{1,0:T(8,128)(2,1)}), bf16[1536,1536]{1,0:T(8,128)(2,1)}) %all-gather.14.cloned.1.call-update) | async-done | bytes 4718608 | tf_op jit(solution)/shard_map/all_gather | solution.py:258
  1203.8 273.3 %while.41 = (s32[]{:T(128)}, f32[1536,6,64]{0,2,1:T(8,128)}, f32[1536,6,64]{0,2,1:T(8,128)}, f32[768,6,64]{0,2,1:T(8,128)}, f32[768,6,64]{0,2,1:T(8,128)}, /*ind...) while((s32[]{:T(128)}, f32[1536,6,64]{0,2,1:T(8,128)}, ...), condition=%wide.region_22.23_spmd.clone, body=%wide.region_19.22_spmd.clone.sunk | while | flops 4605935616 | bytes 376722592 | solution.py:308
  1221.4 9.5 multiply_convert_fusion.12
  1253.7 16.1 multiply_reduce_fusion.14
  1269.8 12.5 multiply_convert_fusion.11
  1311.7 9.5 multiply_convert_fusion.12
  1345.1 16.1 multiply_reduce_fusion.14
  1361.3 12.5 multiply_convert_fusion.11
  1403.1 9.5 multiply_convert_fusion.12
  1436.4 16.1 multiply_reduce_fusion.14
  1452.6 12.5 multiply_convert_fusion.11
  1502.1 157.6 %reduce-scatter.24.cloned.1.call-done = f32[384,1536]{1,0:T(8,128)} async-done(((f32[1536,1536]{1,0:T(8,128)}), f32[384,1536]{1,0:T(8,128)}) %reduce-scatter.24.cloned.1.call-update) | async-done | bytes 2359312 | tf_op jit(solution)/shard_map/reduce_scatter | solution.py:334
  1700.3 9.9 fusion.126
  1710.3 9.9 fusion.125
  1720.3 10.7 fusion.124
  1775.0 63.1 %reduce-scatter.42.cloned.1.call-done = f32[512,384]{0,1:T(8,128)} async-done(((f32[4096,384]{0,1:T(8,128)}), f32[512,384]{0,1:T(8,128)}) %reduce-scatter.42.cloned.1.call-update) | async-done | bytes 786448 | tf_op jit(solution)/shard_map/reduce_scatter | solution.py:379
  1845.9 23.8 %all-reduce = (f32[6,384]{1,0:T(8,128)}, f32[6,64]{1,0:T(8,128)}, f32[6,64]{1,0:T(8,128)}, f32[6,64]{1,0:T(8,128)}, f32[6]{0:T(128)}) all-reduce(f32[6,384]{1,0:T(8,128)S(1)} %copy.64, f32[6,64]{1,0:T(8,128)S(1)} %reduce_sum.224, f32[6,64]{1,0:T(8,128)S(1)} %reduce_sum.226, ...), channel_id=1, replica_groups=mesh['seq'=8,'tp'=4] {'seq'}, use_global_device_ids=true, to_apply=%region_40.41 | all-reduce | flops 3462 | bytes 27696 | tf_op jit(solution)/shard_map/psum | solution.py:384
  1869.8 34.0 %reduce-scatter.38.cloned.1.call-done = f32[1024,192]{0,1:T(8,128)} async-done(((f32[1024,1536]{0,1:T(8,128)}), f32[1024,192]{0,1:T(8,128)}) %reduce-scatter.38.cloned.1.call-update) | async-done | bytes 786448 | tf_op jit(solution)/shard_map/reduce_scatter | solution.py:382
  1903.8 65.9 %reduce-scatter.36.cloned.1.call-done = f32[192,1024]{1,0:T(8,128)} async-done(((f32[1536,1024]{1,0:T(8,128)}), f32[192,1024]{1,0:T(8,128)}) %reduce-scatter.36.cloned.1.call-update) | async-done | bytes 786448 | tf_op jit(solution)/shard_map/reduce_scatter | solution.py:377
  1969.7 65.6 %reduce-scatter.34.cloned.1.call-done = f32[192,1024]{1,0:T(8,128)} async-done(((f32[1536,1024]{1,0:T(8,128)}), f32[192,1024]{1,0:T(8,128)}) %reduce-scatter.34.cloned.1.call-update) | async-done | bytes 786448 | tf_op jit(solution)/shard_map/reduce_scatter | solution.py:376
  2035.3 46.6 %reduce-scatter.32.cloned.1.call-done = f32[384,192]{0,1:T(8,128)} async-done(((f32[384,1536]{0,1:T(8,128)}), f32[384,192]{0,1:T(8,128)}) %reduce-scatter.32.cloned.1.call-update) | async-done | bytes 294928 | tf_op jit(solution)/shard_map/reduce_scatter | solution.py:381
  2082.0 46.3 %reduce-scatter.30.cloned.1.call-done = f32[192,384]{1,0:T(8,128)} async-done(((f32[1536,384]{1,0:T(8,128)}), f32[192,384]{1,0:T(8,128)}) %reduce-scatter.30.cloned.1.call-update) | async-done | bytes 294928 | tf_op jit(solution)/shard_map/reduce_scatter | solution.py:375
  2128.3 46.6 %reduce-scatter.28.cloned.1.call-done = f32[192,384]{1,0:T(8,128)} async-done(((f32[1536,384]{1,0:T(8,128)}), f32[192,384]{1,0:T(8,128)}) %reduce-scatter.28.cloned.1.call-update) | async-done | bytes 294928 | tf_op jit(solution)/shard_map/reduce_scatter | solution.py:374
  2174.9 46.4 %reduce-scatter.26.cloned.1.call-done = f32[192,384]{1,0:T(8,128)} async-done(((f32[1536,384]{1,0:T(8,128)}), f32[192,384]{1,0:T(8,128)}) %reduce-scatter.26.cloned.1.call-update) | async-done | bytes 294928 | tf_op jit(solution)/shard_map/reduce_scatter | solution.py:373
  2221.4 80.8 %reduce-scatter.44.cloned.1.call-done = f32[128,6,384]{2,0,1:T(8,128)} async-done(((f32[1024,6,384]{2,0,1:T(8,128)}), f32[128,6,384]{2,0,1:T(8,128)}) %reduce-scatter.44.cloned.1.call-update) | async-done | bytes 1179664 | tf_op jit(solution)/shard_map/reduce_scatter | solution.py:380
  (492 shorter events, 450.8 us)
Async XLA Ops:
  7.2 811.2 %copy-start = (bf16[1024,1536]{1,0:T(8,128)(2,1)S(1)}, bf16[1024,1536]{1,0:T(8,128)(2,1)}, u32[]{:S(2)}) copy-start(bf16[1024,1536]{1,0:T(8,128)(2,1)} %param.38) | copy-start | bytes 9437188
  7.2 118.5 %all-gather.6.cloned.1.call-start = ((), (), s32[]{:S(2)}) async-start(), calls=%async_computation.15 | async-start | bytes 5898240 | tf_op jit(solution)/shard_map/all_gather | solution.py:125
  10.5 20.2 copy-start.72
  34.8 206.3 %all-gather.8.cloned.1.call-start = ((), (), s32[]{:S(2)}) async-start(), calls=%async_computation.16 | async-start | bytes 7864320 | tf_op jit(solution)/shard_map/all_gather | solution.py:126
  35.5 594.2 %reduce-scatter.18.cloned.1.call-start = ((), (), s32[]{:S(2)}) async-start(), calls=%async_computation.17 | async-start | bytes 11796480 | tf_op jit(solution)/shard_map/reduce_scatter | solution.py:201
  35.9 99.3 %copy-start.78 = (f32[6,64]{1,0:T(8,128)}, f32[6,64]{1,0:T(8,128)S(1)}, u32[]{:S(2)}) copy-start(f32[6,64]{1,0:T(8,128)S(1)} %convert_element_type.132) | copy-start | bytes 4612
  39.4 97.3 %copy-start.50 = (f32[1536,32]{0,1:T(8,128)}, f32[1536,32]{0,1:T(8,128)S(1)}, u32[]{:S(2)}) copy-start(f32[1536,32]{0,1:T(8,128)S(1)} %get-tuple-element.518) | copy-start | bytes 589828
  39.4 97.3 %copy-start.52 = (f32[1536,32]{0,1:T(8,128)}, f32[1536,32]{0,1:T(8,128)S(1)}, u32[]{:S(2)}) copy-start(f32[1536,32]{0,1:T(8,128)S(1)} %get-tuple-element.519) | copy-start | bytes 589828
  142.2 105.5 %copy-start.83 = (f32[6,64]{1,0:T(8,128)S(1)}, f32[6,64]{1,0:T(8,128)}, u32[]{:S(2)}) copy-start(f32[6,64]{1,0:T(8,128)} %convert_element_type.136) | copy-start | bytes 4612
  241.1 7.7 copy-start.23
  241.1 7.7 copy-start.100
  470.0 259.1 %all-gather.10.cloned.1.call-start = ((), (), s32[]{:S(2)}) async-start(), calls=%async_computation.18 | async-start | bytes 5898240 | tf_op jit(solution)/shard_map/all_gather | solution.py:213
  629.7 6.4 copy-start.29
  634.7 462.7 %copy-start.74 = (f32[384]{0:T(512)}, f32[384]{0:T(512)S(1)}, u32[]{:S(2)}) copy-start(f32[384]{0:T(512)S(1)} %add_rsqrt_fusion.3) | copy-start | bytes 4612
  638.7 179.7 %all-gather.12.cloned.1.call-start = ((), (), s32[]{:S(2)}) async-start(), calls=%async_computation.20 | async-start | bytes 5898240 | tf_op jit(solution)/shard_map/all_gather | solution.py:232
  643.1 365.8 %reduce-scatter.22.cloned.1.call-start = ((), (), s32[]{:S(2)}) async-start(), calls=%async_computation.21 | async-start | bytes 11796480 | tf_op jit(solution)/shard_map/reduce_scatter | solution.py:241
  729.1 10.3 copy-start.99
  729.1 10.3 copy-start.101
  818.4 13.9 copy-start.102
  832.3 8.3 copy-start.107
  832.3 8.3 copy-start.103
  849.1 248.3 %reduce-scatter.20.cloned.1.call-start = ((), (), s32[]{:S(2)}) async-start(), calls=%async_computation.19 | async-start | bytes 5898240 | tf_op jit(solution)/shard_map/reduce_scatter | solution.py:220
  857.8 151.2 %copy-start.12 = (f32[384,1536]{1,0:T(8,128)S(1)}, f32[384,1536]{1,0:T(8,128)}, u32[]{:S(2)}) copy-start(f32[384,1536]{1,0:T(8,128)} %copy-done.11) | copy-start | bytes 7077892
  857.8 336.5 %all-gather.14.cloned.1.call-start = ((), (), s32[]{:S(2)}) async-start(), calls=%async_computation.22 | async-start | bytes 5898240 | tf_op jit(solution)/shard_map/all_gather | solution.py:258
  1097.4 6.9 copy-start.90
  1097.4 7.5 copy-start.92
  1104.2 555.5 %reduce-scatter.24.cloned.1.call-start = ((), (), s32[]{:S(2)}) async-start(), calls=%async_computation.23 | async-start | bytes 11796480 | tf_op jit(solution)/shard_map/reduce_scatter | solution.py:334
  1105.6 94.8 %copy-start.95 = (f32[6]{0:T(128)S(1)}, f32[6]{0:T(128)}, u32[]{:S(2)}) copy-start(f32[6]{0:T(128)} %copy-done.94) | copy-start | bytes 76
  1242.9 6.4 copy-start.2
  1333.5 6.4 copy-start.2
  1424.9 6.4 copy-start.2
  1480.8 13.7 copy-start.38
  1499.8 262.5 %reduce-scatter.46.cloned.1.call-start = ((), (), s32[]{:S(2)}) async-start(), calls=%async_computation.34 | async-start | bytes 983040
  1502.1 159.6 %copy-start.16 = (bf16[384,1536]{1,0:T(8,128)(2,1)S(1)}, bf16[384,1536]{1,0:T(8,128)(2,1)}, u32[]{:S(2)}) copy-start(bf16[384,1536]{1,0:T(8,128)(2,1)} %param.26) | copy-start | bytes 3538948
  1502.1 159.6 %copy-start.73 = (f32[384]{0:T(512)S(1)}, f32[384]{0:T(512)}, u32[]{:S(2)}) copy-start(f32[384]{0:T(512)} %copy-done.72) | copy-start | bytes 4612
  1684.0 88.7 %reduce-scatter.40.cloned.1.call-start = ((), (), s32[]{:S(2)}) async-start(), calls=%async_computation.31 | async-start | bytes 7077888 | tf_op jit(solution)/shard_map/reduce_scatter | solution.py:378
  1691.4 146.7 %reduce-scatter.42.cloned.1.call-start = ((), (), s32[]{:S(2)}) async-start(), calls=%async_computation.32 | async-start | bytes 7077888 | tf_op jit(solution)/shard_map/reduce_scatter | solution.py:379
  1700.1 203.7 %reduce-scatter.38.cloned.1.call-start = ((), (), s32[]{:S(2)}) async-start(), calls=%async_computation.30 | async-start | bytes 7077888 | tf_op jit(solution)/shard_map/reduce_scatter | solution.py:382
  1710.3 259.4 %reduce-scatter.36.cloned.1.call-start = ((), (), s32[]{:S(2)}) async-start(), calls=%async_computation.29 | async-start | bytes 7077888 | tf_op jit(solution)/shard_map/reduce_scatter | solution.py:377
  1720.2 315.1 %reduce-scatter.34.cloned.1.call-start = ((), (), s32[]{:S(2)}) async-start(), calls=%async_computation.28 | async-start | bytes 7077888 | tf_op jit(solution)/shard_map/reduce_scatter | solution.py:376
  1731.0 350.9 %reduce-scatter.32.cloned.1.call-start = ((), (), s32[]{:S(2)}) async-start(), calls=%async_computation.27 | async-start | bytes 2654208 | tf_op jit(solution)/shard_map/reduce_scatter | solution.py:381
  1738.8 389.5 %reduce-scatter.30.cloned.1.call-start = ((), (), s32[]{:S(2)}) async-start(), calls=%async_computation.26 | async-start | bytes 2654208 | tf_op jit(solution)/shard_map/reduce_scatter | solution.py:375
  1746.5 428.5 %reduce-scatter.28.cloned.1.call-start = ((), (), s32[]{:S(2)}) async-start(), calls=%async_computation.25 | async-start | bytes 2654208 | tf_op jit(solution)/shard_map/reduce_scatter | solution.py:374
  1754.2 467.2 %reduce-scatter.26.cloned.1.call-start = ((), (), s32[]{:S(2)}) async-start(), calls=%async_computation.24 | async-start | bytes 2654208 | tf_op jit(solution)/shard_map/reduce_scatter | solution.py:373
  1761.9 540.3 %reduce-scatter.44.cloned.1.call-start = ((), (), s32[]{:S(2)}) async-start(), calls=%async_computation.33 | async-start | bytes 10616832 | tf_op jit(solution)/shard_map/reduce_scatter | solution.py:380
  1763.5 6.4 copy-start.35
  1769.9 70.4 %copy-start.17 = (bf16[384,1536]{1,0:T(8,128)(2,1)S(1)}, bf16[384,1536]{1,0:T(8,128)(2,1)}, u32[]{:S(2)}) copy-start(bf16[384,1536]{1,0:T(8,128)(2,1)} %param.26) | copy-start | bytes 3538948
  1843.8 458.4 %copy-start.1 = (bf16[1024,1536]{1,0:T(8,128)(2,1)S(1)}, bf16[1024,1536]{1,0:T(8,128)(2,1)}, u32[]{:S(2)}) copy-start(bf16[1024,1536]{1,0:T(8,128)(2,1)} %param.38) | copy-start | bytes 9437188
  (94 other events, 234.5 us)
Sparse Core Ops, SparseCore 0:
  34.9 90.7 all-gather.5
  127.2 113.7 all-gather.7
  470.2 159.5 reduce-scatter.17
  638.8 90.2 all-gather.9
  730.5 87.8 all-gather.11
  849.2 159.7 reduce-scatter.21
  1011.3 86.0 reduce-scatter.19
  1104.3 89.9 all-gather.13
  1499.9 159.7 reduce-scatter.23
  1684.1 24.1 reduce-scatter.45
  1711.7 60.9 reduce-scatter.39
  1776.3 61.7 reduce-scatter.41
  1842.0 61.7 reduce-scatter.37
  1908.0 61.7 reduce-scatter.35
  1973.5 61.7 reduce-scatter.33
  2039.5 42.4 reduce-scatter.31
  2085.7 42.4 reduce-scatter.29
  2132.4 42.4 reduce-scatter.27
  2178.8 42.4 reduce-scatter.25
  2225.7 76.4 reduce-scatter.43
where the time goes:
time: 2320 us; the launch traced here: 2310 us
  waiting for transfers between devices  1480 us (64%)
  matrix products  438 us (19%)
  local copies, waits for them, and re-layouts  187 us (8%)
  other arithmetic  135 us (6%)
  blocking collectives  39 us (2%)
    reduce_scatter x1, waiting for transfers between devices, body(): lax.psum_scatter(jnp.dot(row_block(grad_query, start, local_rows * lax.ax...  158 us
    reduce_scatter x1, waiting for transfers between devices, body(): lax.psum_scatter(jnp.dot(row_block(mixed, jnp.int32(0), local_rows * lax....  156 us
    reduce_scatter x1, waiting for transfers between devices, body(): lax.psum_scatter(jnp.dot(row_block(grad_gate, start, local_rows * lax.axi...  151 us
    dynamic_update_slice x18, local copies, waits for them, and re-layouts, body(): lax.map(forward_block, block_starts)  110 us
    all_gather x1, waiting for transfers between devices, body(): lax.all_gather(caption, 'tp', axis=0, tiled=True)  98.8 us
    all_gather x1, waiting for transfers between devices, body(): grad_attn_all = lax.all_gather(grad_attn_own, 'tp', axis=0, tiled=True)  88.7 us
    all_gather x1, waiting for transfers between devices, body(): lax.all_gather(outgoing, 'tp', axis=0, tiled=True)  86.3 us
    all_gather x1, waiting for transfers between devices, body(): lax.all_gather((normed_mid * (1.0 + scale_ffn) + shift_ffn).astype(bf_typ...  85.9 us
  transfers between devices with their start and end apart: 20, of which 19 were waited for; matrix products, arithmetic and copies ran while one was open for 6% of the time, Pallas kernels for 0%

commit v1 on v0

v1 whole, which is shorter than its diff:
```python
import functools
import math

import jax
import jax.numpy as jnp
from jax import lax
from jax.experimental import pallas as pl
from jax.experimental.pallas import tpu as pltpu
from jax.sharding import PartitionSpec as P

epsilon = 1e-06
f_type = jnp.float32
bf_type = jnp.bfloat16
BLOCK = 256
LANES = 128
HEAD = 64
MASK = -2048.0
EXP_SCALE = HEAD ** -0.5 / math.log(2.0)
VMEM_LIMIT = 56 * 2**20


def dot_nt(a, b):
    return lax.dot_general(a, b, (((1,), (1,)), ((), ())), preferred_element_type=f_type)


def dot_tn(a, b):
    return lax.dot_general(a, b, (((0,), (0,)), ((), ())), preferred_element_type=f_type)


def dot_nn(a, b):
    return jnp.dot(a, b, preferred_element_type=f_type)


def lane_of(shape):
    return lax.broadcasted_iota(jnp.int32, shape, len(shape) - 1)


def head_mean(x):
    r = lax.broadcasted_iota(jnp.int32, (LANES, LANES), 0) // HEAD
    c = lax.broadcasted_iota(jnp.int32, (LANES, LANES), 1) // HEAD
    ones = jnp.where(r == c, 1.0 / HEAD, 0.0).astype(bf_type)
    high = x.astype(bf_type)
    low = (x - high.astype(f_type)).astype(bf_type)
    return dot_nn(high, ones) + dot_nn(low, ones)


def swap_halves(x):
    lanes = lane_of(x.shape)
    up = pltpu.roll(x, LANES - 32, 1)
    down = pltpu.roll(x, 32, 1)
    return jnp.where((lanes % HEAD) < 32, up, down)


def normed(x):
    factor = lax.rsqrt(head_mean(x * x) + epsilon)
    return x * factor, factor


def split_pair(x):
    first = lane_of(x.shape) < HEAD
    zero = jnp.zeros_like(x)
    return jnp.concatenate([jnp.where(first, x, zero), jnp.where(first, zero, x)], axis=0)


def join_pair(x):
    n = x.shape[0] // 2
    first = lane_of((n, LANES)) < HEAD
    return jnp.where(first, x[:n, :LANES], x[n:, :LANES])


def self_kernel(lo, hi, q_ref, k_ref, v_ref, cos_ref, sin_ref, qg_ref, kg_ref, qm_ref, km_ref,
                qrot_ref, krot_ref, o_ref, il_ref, ke, ve, qe, acc):
    n_blocks = q_ref.shape[0] // BLOCK

    def prepare(i, _):
        rows = pl.ds(pl.multiple_of(i * BLOCK, BLOCK), BLOCK)
        cos, sin = cos_ref[rows, :], sin_ref[rows, :]
        for src, gain, dst in ((q_ref, qg_ref, qrot_ref), (k_ref, kg_ref, krot_ref)):
            hat, _f = normed(src[rows, :])
            x = hat * gain[0]
            dst[rows, :] = (x * cos + swap_halves(x) * sin).astype(bf_type)
        ke[rows, :LANES] = krot_ref[rows, :]
        ke[rows, LANES:] = km_ref[rows, :]
        ve[rows, :LANES] = v_ref[rows, :].astype(bf_type)
        ve[rows, LANES:] = jnp.ones((BLOCK, LANES), bf_type)
        return 0

    lax.fori_loop(0, n_blocks, prepare, 0)

    def one(i, _):
        rows = pl.ds(pl.multiple_of(i * BLOCK, BLOCK), BLOCK)
        qe[:, :LANES] = split_pair(qrot_ref[rows, :])
        qm = qm_ref[rows, :]
        qe[:BLOCK, LANES:] = qm
        qe[BLOCK:, LANES:] = qm
        acc[...] = jnp.zeros_like(acc)

        def step(j, _):
            cols = pl.ds(pl.multiple_of(j * BLOCK, BLOCK), BLOCK)
            s = dot_nt(qe[...], ke[cols, :])
            e = jnp.exp2(s * EXP_SCALE).astype(bf_type)
            acc[...] += dot_nn(e, ve[cols, :])
            return 0

        lax.fori_loop(lo[i], hi[i], step, 0)
        inv = join_pair(1.0 / acc[:, LANES:])
        o_ref[rows, :] = join_pair(acc[:, :LANES]) * inv
        il_ref[rows, :] = inv
        return 0

    lax.fori_loop(0, n_blocks, one, 0)


def cross_kernel(clo, chi, qrot_ref, tk_ref, tv_ref, tg_ref, qm_ref, tm_ref, gate_ref, so_ref,
                 mixed_ref, co_ref, cil_ref, tke, tve, qe, acc, *, per_clip):
    n_blocks = qrot_ref.shape[0] // BLOCK
    n_text = tk_ref.shape[0] // BLOCK

    def prepare(i, _):
        rows = pl.ds(pl.multiple_of(i * BLOCK, BLOCK), BLOCK)
        hat, _f = normed(tk_ref[rows, :])
        tke[rows, :LANES] = (hat * tg_ref[0]).astype(bf_type)
        tke[rows, LANES:] = tm_ref[rows, :]
        tve[rows, :LANES] = tv_ref[rows, :].astype(bf_type)
        tve[rows, LANES:] = jnp.ones((BLOCK, LANES), bf_type)
        return 0

    lax.fori_loop(0, n_text, prepare, 0)

    def one(i, _):
        rows = pl.ds(pl.multiple_of(i * BLOCK, BLOCK), BLOCK)
        qe[:, :LANES] = split_pair(qrot_ref[rows, :])
        qm = qm_ref[rows, :]
        qe[:BLOCK, LANES:] = qm
        qe[BLOCK:, LANES:] = qm
        acc[...] = jnp.zeros_like(acc)

        def step(j, _):
            cols = pl.ds(pl.multiple_of(j * per_clip, per_clip), per_clip)
            s = dot_nt(qe[...], tke[cols, :])
            e = jnp.exp2(s * EXP_SCALE).astype(bf_type)
            acc[...] += dot_nn(e, tve[cols, :])
            return 0

        lax.fori_loop(clo[i], chi[i], step, 0)
        inv = join_pair(1.0 / acc[:, LANES:])
        cross = join_pair(acc[:, :LANES]) * inv
        co_ref[rows, :] = cross
        cil_ref[rows, :] = inv
        mixed_ref[rows, :] = (so_ref[rows, :] + gate_ref[0] * cross).astype(bf_type)
        return 0

    lax.fori_loop(0, n_blocks, one, 0)


def back_kernel(lo, hi, clo, chi,
                qrot_ref, krot_ref, q_ref, k_ref, v_ref, tk_ref, tv_ref, o_ref, il_ref, co_ref, cil_ref,
                gm_ref, gate_ref, cos_ref, sin_ref, qg_ref, kg_ref, tg_ref, qm_ref, km_ref, tm_ref,
                gq_ref, gk_ref, gv_ref, gtk_ref, gtv_ref, dqg_ref, dkg_ref, dtg_ref, dgate_ref,
                ke, ve, tke, tve, qe, ge, ce, dq, dk, dv, dtk, dtv, dqa, *, per_clip, scale):
    n_blocks = qrot_ref.shape[0] // BLOCK
    n_text = tk_ref.shape[0] // BLOCK
    marks = jnp.where(lane_of((BLOCK, LANES)) < 2, 1.0, 0.0).astype(bf_type)

    def prepare(i, _):
        rows = pl.ds(pl.multiple_of(i * BLOCK, BLOCK), BLOCK)
        ke[rows, :LANES] = krot_ref[rows, :]
        ke[rows, LANES:] = km_ref[rows, :]
        ve[rows, :LANES] = v_ref[rows, :].astype(bf_type)
        ve[rows, LANES:] = marks
        dk[rows, :] = jnp.zeros((BLOCK, LANES), f_type)
        dv[rows, :] = jnp.zeros((BLOCK, LANES), f_type)
        return 0

    lax.fori_loop(0, n_blocks, prepare, 0)

    def prepare_text(i, _):
        rows = pl.ds(pl.multiple_of(i * BLOCK, BLOCK), BLOCK)
        hat, _f = normed(tk_ref[rows, :])
        tke[rows, :LANES] = (hat * tg_ref[0]).astype(bf_type)
        tke[rows, LANES:] = tm_ref[rows, :]
        tve[rows, :LANES] = tv_ref[rows, :].astype(bf_type)
        tve[rows, LANES:] = marks
        dtk[rows, :] = jnp.zeros((BLOCK, LANES), f_type)
        dtv[rows, :] = jnp.zeros((BLOCK, LANES), f_type)
        return 0

    lax.fori_loop(0, n_text, prepare_text, 0)
    dgate_ref[...] = jnp.zeros_like(dgate_ref)

    def load_grad(dst, grad, out, inv):
        scaled = (grad * inv).astype(bf_type)
        dst[:, :LANES] = split_pair(scaled)
        delta = head_mean(grad * out) * (-HEAD) * inv
        lanes = lane_of((BLOCK, LANES))
        for h in range(2):
            one = jnp.broadcast_to(delta[:, h * HEAD:h * HEAD + 1], (BLOCK, LANES))
            high = one.astype(bf_type)
            low = (one - high.astype(f_type)).astype(bf_type)
            both = jnp.where(lanes == 0, high, jnp.where(lanes == 1, low, jnp.zeros_like(low)))
            dst[h * BLOCK:(h + 1) * BLOCK, LANES:] = both

    def pair_step(cols, keys, values, grads, dkey, dvalue):
        s = dot_nt(keys[cols, :], qe[...])
        e = jnp.exp2(s * EXP_SCALE)
        dd = dot_nt(values[cols, :], grads[...])
        ds = (e * dd).astype(bf_type)
        dkey[cols, :] += dot_nn(ds, qe[:, :LANES])
        dvalue[cols, :] += dot_nn(e.astype(bf_type), grads[:, :LANES])
        dqa[...] += dot_tn(ds, keys[cols, :LANES])

    def one(i, _):
        rows = pl.ds(pl.multiple_of(i * BLOCK, BLOCK), BLOCK)
        qe[:, :LANES] = split_pair(qrot_ref[rows, :])
        qm = qm_ref[rows, :]
        qe[:BLOCK, LANES:] = qm
        qe[BLOCK:, LANES:] = qm
        gm = gm_ref[rows, :].astype(f_type)
        load_grad(ge, gm, o_ref[rows, :], il_ref[rows, :])
        co = co_ref[rows, :]
        load_grad(ce, gm * gate_ref[0], co, cil_ref[rows, :])
        dgate_ref[0] += jnp.sum(gm * co, axis=0, keepdims=True)
        dqa[...] = jnp.zeros_like(dqa)

        def step(j, _):
            pair_step(pl.ds(pl.multiple_of(j * BLOCK, BLOCK), BLOCK), ke, ve, ge, dk, dv)
            return 0

        lax.fori_loop(lo[i], hi[i], step, 0)

        def cross_step(j, _):
            pair_step(pl.ds(pl.multiple_of(j * per_clip, per_clip), per_clip), tke, tve, ce, dtk, dtv)
            return 0

        lax.fori_loop(clo[i], chi[i], cross_step, 0)
        dq[rows, :] = join_pair(dqa[...])
        return 0

    lax.fori_loop(0, n_blocks, one, 0)
    for d in (dqg_ref, dkg_ref, dtg_ref):
        d[...] = jnp.zeros_like(d)

    def finish(i, _):
        rows = pl.ds(pl.multiple_of(i * BLOCK, BLOCK), BLOCK)
        cos, sin = cos_ref[rows, :], sin_ref[rows, :]
        for grad, pre, gain, dgain, dst in ((dq, q_ref, qg_ref, dqg_ref, gq_ref), (dk, k_ref, kg_ref, dkg_ref, gk_ref)):
            g = grad[rows, :] * scale
            g = g * cos - swap_halves(g) * sin
            hat, factor = normed(pre[rows, :])
            dgain[0] += jnp.sum(g * hat, axis=0, keepdims=True)
            g = g * gain[0]
            dst[rows, :] = (factor * (g - hat * head_mean(g * hat))).astype(bf_type)
        gv_ref[rows, :] = dv[rows, :].astype(bf_type)
        return 0

    lax.fori_loop(0, n_blocks, finish, 0)

    def finish_text(i, _):
        rows = pl.ds(pl.multiple_of(i * BLOCK, BLOCK), BLOCK)
        g = dtk[rows, :] * scale
        hat, factor = normed(tk_ref[rows, :])
        dtg_ref[0] += jnp.sum(g * hat, axis=0, keepdims=True)
        g = g * tg_ref[0]
        gtk_ref[rows, :] = (factor * (g - hat * head_mean(g * hat))).astype(bf_type)
        gtv_ref[rows, :] = dtv[rows, :].astype(bf_type)
        return 0

    lax.fori_loop(0, n_text, finish_text, 0)


def pair_rows(n, at=0):
    return pl.BlockSpec((n, LANES), lambda p, *_: (0, at + p))


def shared_rows(n):
    return pl.BlockSpec((n, LANES), lambda p, *_: (0, 0))


ONE_ROW = pl.BlockSpec((1, 1, LANES), lambda p, *_: (p, 0, 0))


def params():
    return pltpu.CompilerParams(vmem_limit_bytes=VMEM_LIMIT, dimension_semantics=("arbitrary",))


def cost(flops, n_bytes, exps):
    return pl.CostEstimate(flops=int(flops), bytes_accessed=int(n_bytes), transcendentals=int(exps))


def self_attention(lo, hi, qkv, cos, sin, qgain, kgain, qmask, kmask):
    group, pairs = qkv.shape[0], qkv.shape[1] // (3 * LANES)
    spec = pltpu.PrefetchScalarGridSpec(
        num_scalar_prefetch=2, grid=(pairs,),
        in_specs=[pair_rows(group), pair_rows(group, pairs), pair_rows(group, 2 * pairs),
                  shared_rows(group), shared_rows(group), ONE_ROW, ONE_ROW, shared_rows(group), shared_rows(group)],
        out_specs=[pair_rows(group)] * 4,
        scratch_shapes=[pltpu.VMEM((group, 2 * LANES), bf_type), pltpu.VMEM((group, 2 * LANES), bf_type),
                        pltpu.VMEM((2 * BLOCK, 2 * LANES), bf_type), pltpu.VMEM((2 * BLOCK, 2 * LANES), f_type)])
    wide = (group, pairs * LANES)
    return pl.pallas_call(
        self_kernel, grid_spec=spec,
        out_shape=[jax.ShapeDtypeStruct(wide, bf_type), jax.ShapeDtypeStruct(wide, bf_type),
                   jax.ShapeDtypeStruct(wide, f_type), jax.ShapeDtypeStruct(wide, f_type)],
        compiler_params=params(), name="self_attention",
        cost_estimate=cost(pairs * group * group * 8 * HEAD, qkv.size * 8, pairs * group * group),
    )(lo, hi, qkv, qkv, qkv, cos, sin, qgain, kgain, qmask, kmask)


def cross_attention(clo, chi, qrot, tkv, tgain, qmask, tmask, gate, self_out, per_clip):
    group, pairs = qrot.shape[0], qrot.shape[1] // LANES
    text = tkv.shape[0]
    spec = pltpu.PrefetchScalarGridSpec(
        num_scalar_prefetch=2, grid=(pairs,),
        in_specs=[pair_rows(group), pair_rows(text), pair_rows(text, pairs), ONE_ROW,
                  shared_rows(group), shared_rows(text), ONE_ROW, pair_rows(group)],
        out_specs=[pair_rows(group)] * 3,
        scratch_shapes=[pltpu.VMEM((text, 2 * LANES), bf_type), pltpu.VMEM((text, 2 * LANES), bf_type),
                        pltpu.VMEM((2 * BLOCK, 2 * LANES), bf_type), pltpu.VMEM((2 * BLOCK, 2 * LANES), f_type)])
    wide = (group, pairs * LANES)
    return pl.pallas_call(
        functools.partial(cross_kernel, per_clip=per_clip), grid_spec=spec,
        out_shape=[jax.ShapeDtypeStruct(wide, bf_type), jax.ShapeDtypeStruct(wide, f_type),
                   jax.ShapeDtypeStruct(wide, f_type)],
        compiler_params=params(), name="cross_attention",
        cost_estimate=cost(pairs * group * per_clip * 16 * HEAD, qrot.size * 14, pairs * group * per_clip),
    )(clo, chi, qrot, tkv, tkv, tgain, qmask, tmask, gate, self_out)


def attention_back(lo, hi, clo, chi, qrot, krot, qkv, tkv, self_out, inv, cross_out, cinv, gmix, gate,
                   cos, sin, qgain, kgain, tgain, qmask, kmask, tmask, per_clip, scale):
    group, pairs = qrot.shape[0], qrot.shape[1] // LANES
    text = tkv.shape[0]
    spec = pltpu.PrefetchScalarGridSpec(
        num_scalar_prefetch=4, grid=(pairs,),
        in_specs=[pair_rows(group), pair_rows(group),
                  pair_rows(group), pair_rows(group, pairs), pair_rows(group, 2 * pairs),
                  pair_rows(text), pair_rows(text, pairs),
                  pair_rows(group), pair_rows(group), pair_rows(group), pair_rows(group),
                  pair_rows(group), ONE_ROW, shared_rows(group), shared_rows(group), ONE_ROW, ONE_ROW, ONE_ROW,
                  shared_rows(group), shared_rows(group), shared_rows(text)],
        out_specs=[pair_rows(group)] * 3 + [pair_rows(text)] * 2 + [ONE_ROW] * 4,
        scratch_shapes=[pltpu.VMEM((group, 2 * LANES), bf_type), pltpu.VMEM((group, 2 * LANES), bf_type),
                        pltpu.VMEM((text, 2 * LANES), bf_type), pltpu.VMEM((text, 2 * LANES), bf_type),
                        pltpu.VMEM((2 * BLOCK, 2 * LANES), bf_type), pltpu.VMEM((2 * BLOCK, 2 * LANES), bf_type),
                        pltpu.VMEM((2 * BLOCK, 2 * LANES), bf_type),
                        pltpu.VMEM((group, LANES), f_type), pltpu.VMEM((group, LANES), f_type),
                        pltpu.VMEM((group, LANES), f_type), pltpu.VMEM((text, LANES), f_type),
                        pltpu.VMEM((text, LANES), f_type), pltpu.VMEM((2 * BLOCK, LANES), f_type)])
    wide, wide_text = (group, pairs * LANES), (text, pairs * LANES)
    row = jax.ShapeDtypeStruct((pairs, 1, LANES), f_type)
    return pl.pallas_call(
        functools.partial(back_kernel, per_clip=per_clip, scale=scale), grid_spec=spec,
        out_shape=[jax.ShapeDtypeStruct(wide, bf_type)] * 3 + [jax.ShapeDtypeStruct(wide_text, bf_type)] * 2 + [row] * 4,
        compiler_params=params(), name="attention_back",
        cost_estimate=cost(pairs * group * group * 20 * HEAD, qkv.size * 12, pairs * group * group),
    )(lo, hi, clo, chi, qrot, krot, qkv, qkv, qkv, tkv, tkv, self_out, inv, cross_out, cinv, gmix, gate,
      cos, sin, qgain, kgain, tgain, qmask, kmask, tmask)


def rms_parts(values):
    factor = lax.rsqrt(jnp.mean(values * values, axis=-1, keepdims=True) + epsilon)
    return (values * factor, factor)


def rms_back(grad, hat, factor):
    return factor * (grad - hat * jnp.mean(grad * hat, axis=-1, keepdims=True))


def pad_lanes(x, width):
    extra = width - x.shape[-1]
    return x if extra == 0 else jnp.pad(x, [(0, 0)] * (x.ndim - 1) + [(0, extra)])


def lane_rows(gain, pairs):
    flat = gain.astype(f_type).reshape(-1)
    return pad_lanes(flat, pairs * LANES).reshape(pairs, 1, LANES)


def body(tokens, cond_embed, caption, clip_len, rope_off, text_len, query_proj, key_proj, value_proj, out_proj,
         gate_proj, up_proj, down_proj, key_text, value_text, ada_weight, ada_bias, query_gain, key_gain,
         text_gain, text_gate, cotangent):
    tp, seq = lax.axis_size("tp"), lax.axis_size("seq")
    me_tp, me_seq = lax.axis_index("tp"), lax.axis_index("seq")
    own = tokens.shape[0]
    group = own * tp
    width = tokens.shape[1]
    clips = cond_embed.shape[0]
    heads = query_gain.shape[0]
    inner = heads * HEAD
    pairs = -(-inner // LANES)
    wide = pairs * LANES
    text = caption.shape[0] * tp
    per_clip = text // clips
    scale = HEAD ** -0.5

    lengths = clip_len[0]
    order = jnp.arange(clips, dtype=jnp.int32)
    ends = jnp.sum(jnp.where(order[None, :] <= order[:, None], lengths[None, :], 0), axis=1)
    starts = ends - lengths
    row = jnp.arange(group, dtype=jnp.int32)
    member = (row[:, None] >= starts[None, :]) & (row[:, None] < ends[None, :])
    member_int = member.astype(jnp.int32)
    position = jnp.sum(member_int * (row[:, None] - starts[None, :] + rope_off[0][None, :]), axis=1).astype(f_type)
    half = HEAD // 2
    inverse = 10000.0 ** (-jnp.arange(half, dtype=f_type) / half)
    angle = position[:, None] * inverse[None, :]
    cos, sin = jnp.cos(angle), jnp.sin(angle)
    cos = jnp.concatenate([cos] * 4, axis=1)
    sin = jnp.concatenate([-sin, sin, -sin, sin], axis=1)
    lanes = jnp.arange(LANES, dtype=jnp.int32)[None, :]
    clip_row = jnp.sum(member_int * jnp.arange(clips, dtype=jnp.int32)[None, :], axis=1)
    same = clip_row[:, None] == lanes
    qmask = jnp.where(same, MASK, 0.0).astype(bf_type)
    kmask = jnp.where(same, 0.0, 1.0).astype(bf_type)
    t_row = jnp.arange(text, dtype=jnp.int32)
    t_clip = t_row // per_clip
    t_limit = jnp.sum((t_clip[:, None] == jnp.arange(clips)[None, :]) * text_len[0][None, :], axis=1)
    t_valid = t_row - t_clip * per_clip < t_limit
    tmask = jnp.where((t_clip[:, None] == lanes) & t_valid[:, None], 0.0, 1.0).astype(bf_type)
    first = jnp.arange(group // BLOCK, dtype=jnp.int32) * BLOCK
    clo = jnp.sum((first[:, None] >= ends[None, :]).astype(jnp.int32), axis=1)
    last = jnp.sum((first[:, None] + (BLOCK - 1) >= ends[None, :]).astype(jnp.int32), axis=1)
    chi = last + 1
    pick = jnp.arange(clips, dtype=jnp.int32)[None, :]
    lo = jnp.sum(jnp.where(pick == clo[:, None], starts[None, :], 0), axis=1) // BLOCK
    hi = (jnp.sum(jnp.where(pick == last[:, None], ends[None, :], 0), axis=1) + BLOCK - 1) // BLOCK
    own_row = me_tp * own + jnp.arange(own, dtype=jnp.int32)
    own_member = ((own_row[:, None] >= starts[None, :]) & (own_row[:, None] < ends[None, :])).astype(f_type)

    silu_cond = jax.nn.silu(cond_embed.astype(f_type)).astype(bf_type)
    mod_local = jnp.einsum("ck,kjd->cjd", silu_cond, ada_weight, preferred_element_type=f_type) + ada_bias.astype(f_type)[None]
    modulation = lax.all_gather(mod_local, "tp", axis=2, tiled=True)

    def token_mod(which):
        return sum(own_member[:, c:c + 1] * modulation[c, which][None, :] for c in range(clips))

    rows_in = tokens.astype(f_type)
    normed_own, factor_own = rms_parts(rows_in)
    modin_own = (normed_own * (1.0 + token_mod(1)) + token_mod(0)).astype(bf_type)
    modin = lax.all_gather(modin_own, "tp", axis=0, tiled=True)
    text_all = lax.all_gather(caption, "tp", axis=0, tiled=True)

    hid = gate_proj.shape[1] // seq
    gate_slice = lax.dynamic_slice_in_dim(gate_proj, me_seq * hid, hid, 1)
    up_slice = lax.dynamic_slice_in_dim(up_proj, me_seq * hid, hid, 1)
    down_slice = lax.dynamic_slice_in_dim(down_proj, me_seq * hid, hid, 0)
    w_gate = lax.all_gather(gate_slice, "tp", axis=1, tiled=True)
    w_up = lax.all_gather(up_slice, "tp", axis=1, tiled=True)
    w_down = lax.all_gather(down_slice, "tp", axis=0, tiled=True)
    cut = width // seq
    out_slice = lax.dynamic_slice_in_dim(out_proj, me_seq * cut, cut, 1)
    w_out = lax.all_gather(lax.all_gather(out_slice, "tp", axis=0, tiled=True), "seq", axis=1, tiled=True)

    grad_y = cotangent.astype(f_type)
    g_ffn = lax.all_gather((token_mod(5) * grad_y).astype(bf_type), "seq", axis=0, tiled=True)

    qkv_weight = jnp.concatenate([pad_lanes(query_proj, wide), pad_lanes(key_proj, wide), pad_lanes(value_proj, wide)], axis=1)
    tkv_weight = jnp.concatenate([pad_lanes(key_text, wide), pad_lanes(value_text, wide)], axis=1)
    qkv = jnp.dot(modin, qkv_weight, preferred_element_type=f_type)
    qg, kg, tg = (lane_rows(g, pairs) for g in (query_gain, key_gain, text_gain))
    tgate = jnp.tanh(text_gate.astype(f_type))
    gate_rows = lane_rows(jnp.broadcast_to(tgate[:, None], (heads, HEAD)), pairs)
    qrot, krot, self_out, inv = self_attention(lo, hi, qkv, cos, sin, qg, kg, qmask, kmask)
    tkv = jnp.dot(text_all, tkv_weight, preferred_element_type=f_type)
    mixed, cross_out, cinv = cross_attention(clo, chi, qrot, tkv, tg, qmask, tmask, gate_rows, self_out, per_clip)

    mixed_own = lax.all_to_all(mixed[:, :inner], "tp", split_axis=0, concat_axis=1, tiled=True)
    attn_own = jnp.dot(mixed_own, w_out, preferred_element_type=f_type)
    hidden_own = rows_in + token_mod(2) * attn_own
    normed_mid, factor_mid = rms_parts(hidden_own)
    ffn_in = lax.all_gather((normed_mid * (1.0 + token_mod(4)) + token_mod(3)).astype(bf_type), "seq", axis=0, tiled=True)
    gate_pre = jnp.dot(ffn_in, w_gate, preferred_element_type=f_type)
    up_pre = jnp.dot(ffn_in, w_up, preferred_element_type=f_type)
    gate_sig = jax.nn.sigmoid(gate_pre)
    gate_silu = gate_pre * gate_sig
    act = (gate_silu * up_pre).astype(bf_type)
    g_act = dot_nt(g_ffn, w_down)
    g_up = (g_act * gate_silu).astype(bf_type)
    g_gate = (g_act * up_pre * gate_sig * (1.0 + gate_pre * (1.0 - gate_sig))).astype(bf_type)
    g_mid = lax.psum_scatter((dot_nt(g_gate, w_gate) + dot_nt(g_up, w_up)).astype(bf_type), "seq", scatter_dimension=0, tiled=True).astype(f_type)
    ffn_own = lax.psum_scatter(jnp.dot(act, w_down, preferred_element_type=f_type).astype(bf_type), "seq", scatter_dimension=0, tiled=True).astype(f_type)
    output = (hidden_own + token_mod(5) * ffn_own).astype(bf_type)

    d_gate = lax.psum_scatter(dot_tn(ffn_in, g_gate).astype(bf_type), "tp", scatter_dimension=1, tiled=True)
    d_up = lax.psum_scatter(dot_tn(ffn_in, g_up).astype(bf_type), "tp", scatter_dimension=1, tiled=True)
    d_down = lax.psum_scatter(dot_tn(act, g_ffn).astype(bf_type), "tp", scatter_dimension=0, tiled=True)
    d_gate = lax.all_to_all(d_gate, "seq", split_axis=0, concat_axis=1, tiled=True).astype(f_type)
    d_up = lax.all_to_all(d_up, "seq", split_axis=0, concat_axis=1, tiled=True).astype(f_type)
    d_down = lax.all_to_all(d_down, "seq", split_axis=1, concat_axis=0, tiled=True).astype(f_type)

    g_hidden = grad_y + rms_back(g_mid * (1.0 + token_mod(4)), normed_mid, factor_mid)
    g_attn = (token_mod(2) * g_hidden).astype(bf_type)
    d_out = lax.psum_scatter(dot_tn(mixed_own, g_attn).astype(bf_type), "seq", scatter_dimension=1, tiled=True)
    d_out = lax.psum_scatter(d_out, "tp", scatter_dimension=0, tiled=True).astype(f_type)
    g_mixed = lax.all_to_all(dot_nt(g_attn, w_out).astype(bf_type), "tp", split_axis=1, concat_axis=0, tiled=True)

    gq, gk, gv, gtk, gtv, dqg, dkg, dtg, dgate = attention_back(
        lo, hi, clo, chi, qrot, krot, qkv, tkv, self_out, inv, cross_out, cinv, pad_lanes(g_mixed, wide), gate_rows,
        cos, sin, qg, kg, tg, qmask, kmask, tmask, per_clip, scale)
    gq, gk, gv, gtk, gtv = (g[:, :inner] for g in (gq, gk, gv, gtk, gtv))
    g_modin = lax.psum_scatter((dot_nt(gq, query_proj) + dot_nt(gk, key_proj) + dot_nt(gv, value_proj)).astype(bf_type),
                               "tp", scatter_dimension=0, tiled=True).astype(f_type)

    def over_seq(grad):
        return lax.psum_scatter(grad.astype(bf_type), "seq", scatter_dimension=0, tiled=True).astype(f_type)

    d_query, d_key, d_value = (over_seq(dot_tn(modin, g)) for g in (gq, gk, gv))
    d_ktext, d_vtext = (over_seq(dot_tn(text_all, g)) for g in (gtk, gtv))
    grad_tokens = (g_hidden + rms_back(g_modin * (1.0 + token_mod(1)), normed_own, factor_own)).astype(bf_type)

    pieces = (g_modin, g_modin * normed_own, g_hidden * attn_own, g_mid, g_mid * normed_mid, grad_y * ffn_own)
    clip_grad = jnp.stack([jnp.stack([jnp.sum(own_member[:, c:c + 1] * p, axis=0) for p in pieces]) for c in range(clips)])
    g_mod = lax.psum_scatter(clip_grad, "tp", scatter_dimension=2, tiled=True)
    every_mod = lax.all_gather(g_mod, "seq", axis=0, tiled=True)
    every_cond = lax.all_gather(silu_cond, "seq", axis=0, tiled=True)
    span = every_cond.shape[1] // seq
    my_cond = lax.dynamic_slice_in_dim(every_cond, me_seq * span, span, 1).astype(f_type)
    d_adaw = jnp.einsum("ck,cjd->kjd", my_cond, every_mod, precision=lax.Precision.HIGHEST)
    d_adab = jnp.sum(every_mod, axis=0)

    def gains(d):
        return d.reshape(-1)[:inner].reshape(heads, HEAD)

    d_tgate = jnp.sum(gains(dgate), axis=1) * (1.0 - tgate * tgate)
    d_qgain, d_kgain, d_tgain, d_tgate = lax.psum((gains(dqg), gains(dkg), gains(dtg), d_tgate), "seq")
    return (output, grad_tokens, d_query, d_key, d_value, d_out, d_gate, d_up, d_down, d_ktext, d_vtext, d_adaw,
            d_adab, d_qgain, d_kgain, d_tgain, d_tgate)


def solution(mesh):
    rows, cols, rep = P(("seq", "tp"), None), P(None, "tp"), P("seq", None)
    flat = P("tp", None)
    in_specs = (rows, rep, rows, rep, rep, rep, cols, cols, cols, flat, cols, cols, flat, cols, cols,
                P(None, None, "tp"), cols, flat, flat, flat, P("tp"), rows)
    grad = P("seq", "tp")
    out_specs = (rows, rows, grad, grad, grad, P("tp", "seq"), grad, grad, P("tp", "seq"), grad, grad,
                 P("seq", None, "tp"), cols, flat, flat, flat, P("tp"))
    return jax.shard_map(body, mesh=mesh, in_specs=in_specs, out_specs=out_specs, check_vma=False)
```

time: 2320 us -> 1310 us (0.56)
  waiting for transfers between devices: 1480 us -> 720 us
  matrix products: 438 us -> 195 us
  Pallas kernels: 0 us -> 139 us
  local copies, waits for them, and re-layouts: 187 us -> 54.5 us
  other arithmetic: 135 us -> 56.5 us
  blocking collectives: 39 us -> 80 us
  starting transfers between devices: 1.98 us -> 38.4 us
    reduce_scatter x14 -> x10, waiting for transfers between devices: 1050 us -> 315 us  [the longest x5 87.9 us: over_seq(): lax.psum_scatter(grad.astype(bf_type), 'seq', scatter_dimension=0, tiled=...]
    dot_general x75 -> x23, matrix products: 435 us -> 191 us  [the longest x9 70 us: dot_tn(): lax.dot_general(a, b, (((0,), (0,)), ((), ())), preferred_element_type=f_...]
    all_gather x5 -> x8, waiting for transfers between devices: 432 us -> 292 us  [the longest x1 63.3 us: body(): text_all = lax.all_gather(caption, 'tp', axis=0, tiled=True)]
    pallas_call x0 -> x3, Pallas kernels: none -> 139 us  [the longest x1 79.7 us: attention_back(): pl.pallas_call(functools.partial(back_kernel, per_clip=per_clip, scale=sc...]
    dynamic_update_slice x18 -> x0, local copies, waits for them, and re-layouts: 110 us -> none  [body(): lax.map(forward_block, block_starts)]
    all_to_all x0 -> x5, waiting for transfers between devices: none -> 67.9 us  [the longest x1 40 us: body(): lax.all_to_all(mixed[:, :inner], 'tp', split_axis=0, concat_axis=1, tiled...]
    convert_element_type x19 -> x14, other arithmetic: 81 us -> 24.7 us  [the longest x1 5.99 us: body(): (normed_mid * (1.0 + token_mod(4)) + token_mod(3)).astype(bf_type)]
    unnamed x21 -> x26, waiting for transfers between devices: 1.03 us -> 45 us
  transfers between devices with their start and end apart: 20 -> 27, of which waited for: 19 -> 18; matrix products, arithmetic and copies ran while one was open for 6% -> 17% of each run, Pallas kernels for 0% -> 11%
where the time goes in v1:
time: 1310 us; the launch traced here: 1300 us
  waiting for transfers between devices  720 us (55%)
  matrix products  195 us (15%)
  Pallas kernels  139 us (11%)
  blocking collectives  80 us (6%)
  other arithmetic  56.5 us (4%)
  local copies, waits for them, and re-layouts  54.5 us (4%)
  starting transfers between devices  38.4 us (3%)
  between operations  15.2 us (1%)
    reduce_scatter x5, waiting for transfers between devices, over_seq(): lax.psum_scatter(grad.astype(bf_type), 'seq', scatter_dimension=0, tiled=...  87.9 us
    reduce_scatter x1, waiting for transfers between devices, body(): lax.psum_scatter((dot_nt(gq, query_proj) + dot_nt(gk, key_proj) + dot_nt(...  85 us
    pallas_call x1, Pallas kernels, attention_back(): pl.pallas_call(functools.partial(back_kernel, per_clip=per_clip, scale=sc...  79.7 us
    reduce_scatter x1, waiting for transfers between devices, body(): lax.psum_scatter(jnp.dot(act, w_down, preferred_element_type=f_type).asty...  75.7 us
    dot_general x9, matrix products, dot_tn(): lax.dot_general(a, b, (((0,), (0,)), ((), ())), preferred_element_type=f_...  70 us
    reduce_scatter x1, waiting for transfers between devices, body(): lax.psum_scatter((dot_nt(g_gate, w_gate) + dot_nt(g_up, w_up)).astype(bf_...  66.4 us
    all_gather x1, waiting for transfers between devices, body(): text_all = lax.all_gather(caption, 'tp', axis=0, tiled=True)  63.3 us
    dot_general x7, matrix products, dot_nt(): lax.dot_general(a, b, (((1,), (1,)), ((), ())), preferred_element_type=f_...  60.2 us
  transfers between devices with their start and end apart: 27, of which 18 were waited for; matrix products, arithmetic and copies ran while one was open for 17% of the time, Pallas kernels for 11%

profile of v1, /device:TPU:0, one launch (start us, length us, event | category | flops | bytes accessed | tf_op | source)
XLA Modules:
  0.0 1298.3 jit_solution(11160380204879707336)
XLA Ops:
  14.5 15.2 %all_gather.36 = f32[3,6,1536]{2,0,1:T(4,128)S(1)} all-gather(f32[3,6,384]{2,0,1:T(4,128)S(1)} %convolution_add_fusion.2), channel_id=1, replica_groups=mesh['seq'=8,'tp'=4] {'tp'}, dimensions={2}, use_global_device_ids=true | all-gather | bytes 138240 | tf_op jit(solution)/shard_map/all_gather | solution.py:432
  35.8 20.4 %all_gather.39 = bf16[1536,192]{0,1:T(8,128)(2,1)} all-gather(bf16[384,192]{0,1:T(8,128)(2,1)S(1)} %copy.110), channel_id=1, replica_groups=mesh['seq'=8,'tp'=4] {'tp'}, dimensions={0}, use_global_device_ids=true | all-gather | bytes 737280 | tf_op jit(solution)/shard_map/all_gather | solution.py:452
  73.2 53.8 %all-gather.10.cloned.1.call-done = bf16[1536,1536]{1,0:T(8,128)(2,1)} async-done(((bf16[384,1536]{1,0:T(8,128)(2,1)}), bf16[1536,1536]{1,0:T(8,128)(2,1)}) %all-gather.10.cloned.1.call-update) | async-done | bytes 4718608 | tf_op jit(solution)/shard_map/all_gather | solution.py:440
  127.0 11.1 fusion.8.q_ref.k_ref.v_ref
  138.2 41.7 %self_attention.1 = (bf16[1536,384]{1,0:T(8,128)(2,1)}, bf16[1536,384]{1,0:T(8,128)(2,1)}, f32[1536,384]{1,0:T(8,128)}, f32[1536,384]{1,0:T(8,128)}) custom-call(s32[6]{0:T(128)} %and_select_fusion.1.lo, s32[6]{0:T(128)} %and_select_fusion.hi, f32[1536,1152]{1,0:T(8,128)} %fusion.8.q_ref.k_ref.v_ref, f32[1536,1152]{1,0:T(8,128)} %fusion.8.q_ref.k_ref.v_ref, ...), custom_call_target="tpu_custom_call" | custom-call | flops 3623878656 | bytes 14155776 | tf_op jit(solution)/shard_map/self_attention/pallas_call | solution.py:300
  179.8 63.3 %all-gather.12.cloned.1.call-done = bf16[768,4096]{1,0:T(8,128)(2,1)} async-done(((bf16[192,4096]{1,0:T(8,128)(2,1)}), bf16[768,4096]{1,0:T(8,128)(2,1)}) %all-gather.12.cloned.1.call-update) | async-done | bytes 6291472 | tf_op jit(solution)/shard_map/all_gather | solution.py:441
  243.1 11.1 fusion.34.tk_ref.tv_ref
  254.2 17.2 %cross_attention.1 = (bf16[1536,384]{1,0:T(8,128)(2,1)}, f32[1536,384]{1,0:T(8,128)}, f32[1536,384]{1,0:T(8,128)}) custom-call(s32[6]{0:T(128)} %copy-done.25, s32[6]{0:T(128)} %broadcast_add_fusion.chi, bf16[1536,384]{1,0:T(8,128)(2,1)} %get-tuple-element.33.qrot_ref, f32[768,768]{1,0:T(8,128)} %fusion.34.tk_ref.tv_ref, f32[768,768]{1,0:T(8,128)} %fusion.34.tk_ref.tv_ref, ...), custom_call_target="tpu_custom_call" | custom-call | flops 1207959552 | bytes 8257536 | tf_op jit(solution)/shard_map/cross_attention/pallas_call | solution.py:320
  282.2 40.0 %all-to-all-done = bf16[4,384,384]{1,2,0:T(8,128)(2,1)} async-done(((bf16[4,384,384]{1,2,0:T(8,128)(2,1)}), bf16[4,384,384]{1,2,0:T(8,128)(2,1)}, u32[]{:S(2)}, u32[]{:S(2)}) %all-to-all-start) | async-done | bytes 1179680 | tf_op jit(solution)/shard_map/all_to_all | solution.py:467
  322.3 7.2 multiply_reduce_fusion.13
  329.6 6.0 add_convert_fusion.1
  340.6 55.3 %all-gather.16.cloned.1.call-done = bf16[3072,1536]{1,0:T(8,128)(2,1)} async-done(((bf16[384,1536]{1,0:T(8,128)(2,1)}), bf16[3072,1536]{1,0:T(8,128)(2,1)}) %all-gather.16.cloned.1.call-update) | async-done | bytes 9437200 | tf_op jit(solution)/shard_map/all_gather | solution.py:471
  395.9 9.8 fusion.58
  405.7 30.0 %all-gather.18.cloned.1.call-done = bf16[1536,512]{1,0:T(8,128)(2,1)} async-done(((bf16[1536,128]{1,0:T(8,128)(2,1)}), bf16[1536,512]{1,0:T(8,128)(2,1)}) %all-gather.18.cloned.1.call-update) | async-done | bytes 1572880 | tf_op jit(solution)/shard_map/all_gather | solution.py:447
  435.6 9.8 fusion.57
  445.4 27.2 %all-gather.22.cloned.1.call-done = bf16[512,1536]{1,0:T(8,128)(2,1)} async-done(((bf16[128,1536]{1,0:T(8,128)(2,1)}), bf16[512,1536]{1,0:T(8,128)(2,1)}) %all-gather.22.cloned.1.call-update) | async-done | bytes 1572880 | tf_op jit(solution)/shard_map/all_gather | solution.py:449
  472.6 60.2 %all-gather.24.cloned.1.call-done = bf16[3072,1536]{1,0:T(8,128)(2,1)} async-done(((bf16[384,1536]{1,0:T(8,128)(2,1)}), bf16[3072,1536]{1,0:T(8,128)(2,1)}) %all-gather.24.cloned.1.call-update) | async-done | bytes 9437200 | tf_op jit(solution)/shard_map/all_gather | solution.py:455
  532.7 14.9 %multiply_convert_fusion = (bf16[3072,512]{1,0:T(8,128)(2,1)S(1)}, bf16[3072,512]{1,0:T(8,128)(2,1)S(1)}, bf16[3072,512]{1,0:T(8,128)(2,1)}) fusion(f32[3072,512]{1,0:T(8,128)} %fusion.57, f32[3072,512]{1,0:T(8,128)} %fusion.58, bf16[3072,1536]{1,0:T(8,128)(2,1)} %all-gather.24.cloned.1.call-done, bf16[512,1536]{1,0:T(8,128)(2,1)} %all-gather.22.cloned.1.call-done), kind=kOutput, calls=%fused_computation.10 | convolution fusion | flops 4855431168 | bytes 33030144 | tf_op jit(solution)/shard_map/dot_general | solution.py:23
  547.7 9.3 fusion.59
  557.0 11.7 add_convert_fusion
  568.9 10.0 convolution_convert_fusion
  579.0 66.4 %reduce-scatter.25.cloned.1.call-done = bf16[384,1536]{1,0:T(8,128)(2,1)} async-done(((bf16[3072,1536]{1,0:T(8,128)(2,1)}), bf16[384,1536]{1,0:T(8,128)(2,1)}) %reduce-scatter.25.cloned.1.call-update) | async-done | bytes 1179664 | tf_op jit(solution)/shard_map/reduce_scatter | solution.py:480
  649.5 75.7 %reduce-scatter.23.cloned.1.call-done = bf16[384,1536]{1,0:T(8,128)(2,1)} async-done(((bf16[3072,1536]{1,0:T(8,128)(2,1)}), bf16[384,1536]{1,0:T(8,128)(2,1)}) %reduce-scatter.23.cloned.1.call-update) | async-done | bytes 1179664 | tf_op jit(solution)/shard_map/reduce_scatter | solution.py:481
  731.1 6.0 convolution_convert_fusion.1
  737.2 10.4 convolution_convert_fusion.4
  747.9 9.5 convolution_convert_fusion.5
  770.6 10.5 convolution_convert_fusion.6
  784.3 15.2 %all-to-all-done.1 = bf16[384,4,384]{2,0,1:T(8,128)(2,1)} async-done(((bf16[384,4,384]{2,0,1:T(8,128)(2,1)}), bf16[384,4,384]{2,0,1:T(8,128)(2,1)}, u32[]{:S(2)}, u32[]{:S(2)}) %all-to-all-start.1) | async-done | bytes 1179680 | tf_op jit(solution)/shard_map/all_to_all | solution.py:495
  799.5 79.7 %attention_back.1 = (bf16[1536,384]{1,0:T(8,128)(2,1)}, bf16[1536,384]{1,0:T(8,128)(2,1)}, bf16[1536,384]{1,0:T(8,128)(2,1)}, bf16[768,384]{1,0:T(8,128)(2,1)}, ...) custom-call(s32[6]{0:T(128)} %and_select_fusion.1.lo, ...), custom_call_target="tpu_custom_call" | custom-call | flops 9059696640 | bytes 21233664 | tf_op jit(solution)/shard_map/attention_back/pallas_call | solution.py:351
  879.2 6.4 convolution_convert_fusion.9
  885.6 6.4 convolution_convert_fusion.8
  892.2 6.4 convolution_convert_fusion.7
  898.7 7.1 fusion.6
  906.9 7.1 fusion.7
  914.0 8.0 fusion.60
  924.3 7.4 convolution_add_fusion.1
  938.1 19.8 %all-to-all-start.4 = ((bf16[128,8,192]{0,2,1:T(8,128)(2,1)}), bf16[128,8,192]{0,2,1:T(8,128)(2,1)S(1)}, u32[]{:S(2)}, u32[]{:S(2)}) async-start(bf16[128,8,192]{0,2,1:T(8,128)(2,1)} %bitcast.17), calls=%async_computation.12 | async-start | bytes 786432 | tf_op jit(solution)/shard_map/all_to_all | solution.py:489
  959.9 6.4 all-to-all-done.4
  969.8 11.7 all-gather
  989.5 6.3 all-to-all-done.2
  1004.1 23.3 %all-reduce = (f32[6,64]{1,0:T(8,128)}, f32[6,64]{1,0:T(8,128)}, f32[6,64]{1,0:T(8,128)}, f32[6]{0:T(128)}) all-reduce(f32[6,64]{1,0:T(8,128)S(1)} %reshape_reshape.34, f32[6,64]{1,0:T(8,128)S(1)} %reshape_reshape.35, f32[6,64]{1,0:T(8,128)S(1)} %reshape_reshape.36, ...), channel_id=1, replica_groups=mesh['seq'=8,'tp'=4] {'seq'}, use_global_device_ids=true, to_apply=%region_45.46 | all-reduce | flops 1158 | bytes 9264 | tf_op jit(solution)/shard_map/psum | solution.py:525
  1032.4 39.9 %reduce-scatter.39.cloned.1.call-done = bf16[512,384]{0,1:T(8,128)(2,1)} async-done(((bf16[4096,384]{0,1:T(8,128)(2,1)}), bf16[512,384]{0,1:T(8,128)(2,1)}) %reduce-scatter.39.cloned.1.call-update) | async-done | bytes 393232 | tf_op jit(solution)/shard_map/reduce_scatter | solution.py:505
  1074.3 48.0 %reduce-scatter.41.cloned.1.call-done = bf16[512,384]{0,1:T(8,128)(2,1)} async-done(((bf16[4096,384]{0,1:T(8,128)(2,1)}), bf16[512,384]{0,1:T(8,128)(2,1)}) %reduce-scatter.41.cloned.1.call-update) | async-done | bytes 393232 | tf_op jit(solution)/shard_map/reduce_scatter | solution.py:505
  1124.3 24.0 %reduce-scatter.43.cloned.1.call-done = bf16[384,192]{1,0:T(8,128)(2,1)} async-done(((bf16[1536,192]{1,0:T(8,128)(2,1)}), bf16[384,192]{1,0:T(8,128)(2,1)}) %reduce-scatter.43.cloned.1.call-update) | async-done | bytes 147472
  1150.2 85.0 %reduce-scatter.27.cloned.1.call-done = bf16[384,1536]{1,0:T(8,128)(2,1)} async-done(((bf16[1536,1536]{1,0:T(8,128)(2,1)}), bf16[384,1536]{1,0:T(8,128)(2,1)}) %reduce-scatter.27.cloned.1.call-update) | async-done | bytes 1179664 | tf_op jit(solution)/shard_map/reduce_scatter | solution.py:501
  1235.2 5.8 multiply_reduce_fusion.11
  1255.2 19.2 %reduce-scatter.49.cloned.1.call-done = f32[384,18]{1,0:T(8,128)} async-done(((f32[1536,18]{1,0:T(8,128)}), f32[384,18]{1,0:T(8,128)}) %reduce-scatter.49.cloned.1.call-update) | async-done | bytes 27664
  1278.7 9.5 all_gather.47
  (234 shorter events, 136.9 us)
Async XLA Ops:
  7.2 271.1 %copy-start = (bf16[1536,1024]{1,0:T(8,128)(2,1)S(1)}, bf16[1536,1024]{1,0:T(8,128)(2,1)}, u32[]{:S(2)}) copy-start(bf16[1536,1024]{1,0:T(8,128)(2,1)} %param.33) | copy-start | bytes 9437188
  7.2 119.8 %all-gather.10.cloned.1.call-start = ((), (), s32[]{:S(2)}) async-start(), calls=%async_computation.19 | async-start | bytes 5898240 | tf_op jit(solution)/shard_map/all_gather | solution.py:440
  10.4 20.1 %copy-start.20 = (f32[384]{0:T(512)}, f32[384]{0:T(512)S(1)}, u32[]{:S(2)}) copy-start(f32[384]{0:T(512)S(1)} %add_rsqrt_fusion.1) | copy-start | bytes 4612
  11.2 19.3 %copy-start.4 = (bf16[384,1536]{1,0:T(8,128)(2,1)S(1)}, bf16[384,1536]{1,0:T(8,128)(2,1)}, u32[]{:S(2)}) copy-start(bf16[384,1536]{1,0:T(8,128)(2,1)} %param.22) | copy-start | bytes 3538948
  11.2 19.3 %copy-start.5 = (bf16[384,1536]{1,0:T(8,128)(2,1)S(1)}, bf16[384,1536]{1,0:T(8,128)(2,1)}, u32[]{:S(2)}) copy-start(bf16[384,1536]{1,0:T(8,128)(2,1)} %param.43) | copy-start | bytes 3538948
  33.7 209.4 %all-gather.12.cloned.1.call-start = ((), (), s32[]{:S(2)}) async-start(), calls=%async_computation.20 | async-start | bytes 7864320 | tf_op jit(solution)/shard_map/all_gather | solution.py:441
  34.5 247.7 %all-gather.14.cloned.1.call-start = ((), (), s32[]{:S(2)}) async-start(), calls=%async_computation.21 | async-start | bytes 5308416 | tf_op jit(solution)/shard_map/all_gather | solution.py:452
  62.7 9.4 copy-start.25
  273.8 48.5 %copy-start.22 = (f32[1536]{0:T(1024)S(1)}, f32[1536]{0:T(1024)}, u32[]{:S(2)}) copy-start(f32[1536]{0:T(1024)} %get-tuple-element.186) | copy-start | bytes 18436
  273.8 48.5 %copy-start.23 = (f32[1536]{0:T(1024)S(1)}, f32[1536]{0:T(1024)}, u32[]{:S(2)}) copy-start(f32[1536]{0:T(1024)} %get-tuple-element.187) | copy-start | bytes 18436
  273.8 48.5 %copy-start.24 = (f32[1536]{0:T(1024)S(1)}, f32[1536]{0:T(1024)}, u32[]{:S(2)}) copy-start(f32[1536]{0:T(1024)} %get-tuple-element.188) | copy-start | bytes 18436
  273.8 48.5 %all-to-all-start = ((bf16[4,384,384]{1,2,0:T(8,128)(2,1)}), bf16[4,384,384]{1,2,0:T(8,128)(2,1)}, u32[]{:S(2)}, u32[]{:S(2)}) async-start(bf16[4,384,384]{1,2,0:T(8,128)(2,1)} %copy.89), calls=%async_computation | async-start | bytes 2359296 | tf_op jit(solution)/shard_map/all_to_all | solution.py:467
  278.2 62.4 %all-gather.20.cloned.1.call-start = ((), (), s32[]{:S(2)}) async-start(), calls=%async_computation.24 | async-start | bytes 1966080 | tf_op jit(solution)/shard_map/all_gather | solution.py:448
  279.2 116.7 %all-gather.16.cloned.1.call-start = ((), (), s32[]{:S(2)}) async-start(), calls=%async_computation.22 | async-start | bytes 10616832 | tf_op jit(solution)/shard_map/all_gather | solution.py:471
  335.6 100.0 %all-gather.18.cloned.1.call-start = ((), (), s32[]{:S(2)}) async-start(), calls=%async_computation.23 | async-start | bytes 1966080 | tf_op jit(solution)/shard_map/all_gather | solution.py:447
  337.5 135.1 %all-gather.22.cloned.1.call-start = ((), (), s32[]{:S(2)}) async-start(), calls=%async_computation.25 | async-start | bytes 1966080 | tf_op jit(solution)/shard_map/all_gather | solution.py:449
  339.3 193.4 %all-gather.24.cloned.1.call-start = ((), (), s32[]{:S(2)}) async-start(), calls=%async_computation.27 | async-start | bytes 10616832 | tf_op jit(solution)/shard_map/all_gather | solution.py:455
  340.1 305.3 %reduce-scatter.25.cloned.1.call-start = ((), (), s32[]{:S(2)}) async-start(), calls=%async_computation.28 | async-start | bytes 10616832 | tf_op jit(solution)/shard_map/reduce_scatter | solution.py:480
  532.7 14.9 %copy-start.29 = (bf16[1536,512]{1,0:T(8,128)(2,1)S(1)}, bf16[1536,512]{1,0:T(8,128)(2,1)}, u32[]{:S(2)}) copy-start(bf16[1536,512]{1,0:T(8,128)(2,1)} %all-gather.18.cloned.1.call-done) | copy-start | bytes 4718596
  547.6 9.4 copy-start.30
  547.6 9.4 copy-start.31
  547.6 9.4 copy-start.28
  568.7 156.5 %reduce-scatter.23.cloned.1.call-start = ((), (), s32[]{:S(2)}) async-start(), calls=%async_computation.26 | async-start | bytes 10616832 | tf_op jit(solution)/shard_map/reduce_scatter | solution.py:481
  578.9 343.1 %reduce-scatter.35.cloned.1.call-start = ((), (), s32[]{:S(2)}) async-start(), calls=%async_computation.33 | async-start | bytes 5308416 | tf_op jit(solution)/shard_map/reduce_scatter | solution.py:493
  737.1 10.8 copy-start.32
  737.1 199.0 %reduce-scatter.37.cloned.1.call-start = ((), (), s32[]{:S(2)}) async-start(), calls=%async_computation.34 | async-start | bytes 1966080 | tf_op jit(solution)/shard_map/reduce_scatter | solution.py:486
  747.7 210.3 %reduce-scatter.47.cloned.1.call-start = ((), (), s32[]{:S(2)}) async-start(), calls=%async_computation.39 | async-start | bytes 1966080
  765.9 33.6 %all-to-all-start.1 = ((bf16[384,4,384]{2,0,1:T(8,128)(2,1)}), bf16[384,4,384]{2,0,1:T(8,128)(2,1)}, u32[]{:S(2)}, u32[]{:S(2)}) async-start(bf16[384,4,384]{2,0,1:T(8,128)(2,1)} %bitcast.108), calls=%async_computation.3 | async-start | bytes 2359296 | tf_op jit(solution)/shard_map/all_to_all | solution.py:495
  770.6 211.5 %reduce-scatter.45.cloned.1.call-start = ((), (), s32[]{:S(2)}) async-start(), calls=%async_computation.38 | async-start | bytes 1966080
  783.8 243.6 %reduce-scatter.29.cloned.1.call-start = ((), (), s32[]{:S(2)}) async-start(), calls=%async_computation.30 | async-start | bytes 1327104 | tf_op jit(solution)/shard_map/reduce_scatter | solution.py:505
  885.6 143.4 %reduce-scatter.31.cloned.1.call-start = ((), (), s32[]{:S(2)}) async-start(), calls=%async_computation.31 | async-start | bytes 1327104 | tf_op jit(solution)/shard_map/reduce_scatter | solution.py:505
  892.1 138.6 %reduce-scatter.33.cloned.1.call-start = ((), (), s32[]{:S(2)}) async-start(), calls=%async_computation.32 | async-start | bytes 1327104 | tf_op jit(solution)/shard_map/reduce_scatter | solution.py:505
  898.6 173.6 %reduce-scatter.39.cloned.1.call-start = ((), (), s32[]{:S(2)}) async-start(), calls=%async_computation.35 | async-start | bytes 3538944 | tf_op jit(solution)/shard_map/reduce_scatter | solution.py:505
  905.8 216.5 %reduce-scatter.41.cloned.1.call-start = ((), (), s32[]{:S(2)}) async-start(), calls=%async_computation.36 | async-start | bytes 3538944 | tf_op jit(solution)/shard_map/reduce_scatter | solution.py:505
  914.0 234.4 %reduce-scatter.43.cloned.1.call-start = ((), (), s32[]{:S(2)}) async-start(), calls=%async_computation.37 | async-start | bytes 983040
  924.2 310.9 %reduce-scatter.27.cloned.1.call-start = ((), (), s32[]{:S(2)}) async-start(), calls=%async_computation.29 | async-start | bytes 5898240 | tf_op jit(solution)/shard_map/reduce_scatter | solution.py:501
  924.3 7.4 copy-start.6
  936.2 33.6 %copy-start.19 = (bf16[3,1024]{1,0:T(4,128)(2,1)S(1)}, bf16[3,1024]{1,0:T(4,128)(2,1)}, u32[]{:S(2)}) copy-start(bf16[3,1024]{1,0:T(4,128)(2,1)} %param.23) | copy-start | bytes 18436
  938.1 28.1 %all-to-all-start.4 = ((bf16[128,8,192]{0,2,1:T(8,128)(2,1)}), bf16[128,8,192]{0,2,1:T(8,128)(2,1)S(1)}, u32[]{:S(2)}, u32[]{:S(2)}) async-start(bf16[128,8,192]{0,2,1:T(8,128)(2,1)} %bitcast.17), calls=%async_computation.12 | async-start | bytes 786432 | tf_op jit(solution)/shard_map/all_to_all | solution.py:489
  966.3 17.7 %all-to-all-start.3 = ((bf16[8,192,128]{2,1,0:T(8,128)(2,1)}), bf16[8,192,128]{2,1,0:T(8,128)(2,1)S(1)}, u32[]{:S(2)}, u32[]{:S(2)}) async-start(bf16[8,192,128]{2,1,0:T(8,128)(2,1)} %bitcast.15), calls=%async_computation.10 | async-start | bytes 786432 | tf_op jit(solution)/shard_map/all_to_all | solution.py:488
  984.0 19.1 %copy-start.27 = (f32[3,1,128]{2,1,0:T(1,128)S(1)}, f32[3,1,128]{2,1,0:T(1,128)}, u32[]{:S(2)}) copy-start(f32[3,1,128]{2,1,0:T(1,128)} %get-tuple-element.48) | copy-start | bytes 4612
  984.0 11.7 all-to-all-start.2
  987.5 287.0 %reduce-scatter.49.cloned.1.call-start = ((), (), s32[]{:S(2)}) async-start(), calls=%async_computation.40 | async-start | bytes 983040
  996.7 238.5 %copy-start.11 = (f32[1536]{0:T(1024)S(1)}, f32[1536]{0:T(1024)}, u32[]{:S(2)}) copy-start(f32[1536]{0:T(1024)} %copy-done.10) | copy-start | bytes 18436
  996.7 238.5 %copy-start.13 = (f32[1536]{0:T(1024)S(1)}, f32[1536]{0:T(1024)}, u32[]{:S(2)}) copy-start(f32[1536]{0:T(1024)} %copy-done.12) | copy-start | bytes 18436
  996.7 238.5 %copy-start.15 = (f32[1536]{0:T(1024)S(1)}, f32[1536]{0:T(1024)}, u32[]{:S(2)}) copy-start(f32[1536]{0:T(1024)} %copy-done.14) | copy-start | bytes 18436
  996.7 238.5 %copy-start.21 = (f32[384]{0:T(512)S(1)}, f32[384]{0:T(512)}, u32[]{:S(2)}) copy-start(f32[384]{0:T(512)} %copy-done.20) | copy-start | bytes 4612
  1250.5 40.8 %copy-start.1 = (bf16[1536,1024]{1,0:T(8,128)(2,1)S(1)}, bf16[1536,1024]{1,0:T(8,128)(2,1)}, u32[]{:S(2)}) copy-start(bf16[1536,1024]{1,0:T(8,128)(2,1)} %param.33) | copy-start | bytes 9437188
  (12 other events, 56.2 us)
Sparse Core Ops, SparseCore 0:
  33.9 93.1 all-gather.9
  128.6 114.4 all-gather.11
  245.0 37.1 all-gather.13
  284.2 49.1 all-gather.19
  335.7 60.1 all-gather.15
  397.9 37.6 all-gather.17
  437.2 35.3 all-gather.21
  475.0 57.6 all-gather.23
  568.8 76.4 reduce-scatter.24
  648.7 76.4 reduce-scatter.22
  737.3 53.8 reduce-scatter.34
  793.4 35.2 reduce-scatter.36
  831.1 34.2 reduce-scatter.46
  867.7 34.2 reduce-scatter.44
  906.0 35.7 reduce-scatter.28
  944.9 37.5 reduce-scatter.30
  985.9 36.7 reduce-scatter.32
  1026.0 46.2 reduce-scatter.38
  1076.0 46.2 reduce-scatter.40
  1125.0 23.2 reduce-scatter.42
  1150.7 84.4 reduce-scatter.26
  1250.6 23.8 reduce-scatter.48

commit v2 on v1

--- a/solution.py
+++ b/solution.py
@@ -355,6 +355,799 @@
         cost_estimate=cost(pairs * group * group * 20 * HEAD, qkv.size * 12, pairs * group * group),
     )(lo, hi, clo, chi, qrot, krot, qkv, qkv, qkv, tkv, tkv, self_out, inv, cross_out, cinv, gmix, gate,
       cos, sin, qgain, kgain, tgain, qmask, kmask, tmask)
+
+
+MESH = pl.DeviceIdType.MESH
+
+
+def meet(peers):
+    barrier = pltpu.get_barrier_semaphore()
+    count = jnp.int32(0)
+    for device, there in peers:
+        if there is None:
+            pl.semaphore_signal(barrier, inc=1, device_id=device, device_id_type=MESH)
+            count += 1
+        else:
+            @pl.when(there)
+            def _(device=device):
+                pl.semaphore_signal(barrier, inc=1, device_id=device, device_id_type=MESH)
+            count += there.astype(jnp.int32)
+    pl.semaphore_wait(barrier, count)
+
+
+def remote(src, dst, send, recv, device):
+    return pltpu.make_async_remote_copy(src_ref=src, dst_ref=dst, send_sem=send, recv_sem=recv,
+                                        device_id=device, device_id_type=MESH)
+
+
+def comm_params(collective_id):
+    return pltpu.CompilerParams(vmem_limit_bytes=VMEM_LIMIT, collective_id=collective_id, has_side_effects=True)
+
+
+def in_vmem(count):
+    return [pl.BlockSpec(memory_space=pltpu.VMEM)] * count
+
+
+def small_gather(arrays, axis, n, collective_id):
+    m = len(arrays)
+
+    def kernel(*refs):
+        x_refs, o_refs, (send, recv) = refs[:m], refs[m:2 * m], refs[2 * m:]
+        me = lax.axis_index(axis)
+        others = [lax.rem(me + d, n) for d in range(1, n)]
+        meet([({axis: o}, None) for o in others])
+        copies = [remote(x_ref, o_ref.at[me], send.at[i, d], recv.at[i, d], {axis: o})
+                  for i, (x_ref, o_ref) in enumerate(zip(x_refs, o_refs)) for d, o in enumerate(others)]
+        for c in copies:
+            c.start()
+        for x_ref, o_ref in zip(x_refs, o_refs):
+            o_ref[me] = x_ref[...]
+        for c in copies:
+            c.wait()
+
+    return pl.pallas_call(
+        kernel, out_shape=[jax.ShapeDtypeStruct((n, *x.shape), x.dtype) for x in arrays],
+        in_specs=in_vmem(m), out_specs=in_vmem(m),
+        scratch_shapes=[pltpu.SemaphoreType.DMA((m, n - 1))] * 2,
+        compiler_params=comm_params(collective_id), name=f"small_gather_{axis}_{collective_id}")(*arrays)
+
+
+def gather_project(x, weights, n, collective_id):
+    own, width = x.shape
+    parts = [w.shape[1] for w in weights]
+
+    def kernel(x_ref, *refs):
+        w_refs, (all_ref, y_ref, send, recv) = refs[:len(weights)], refs[len(weights):]
+        z = lax.axis_index("tp")
+        more, less = z + 1 < n, z > 0
+        meet([({"tp": z + 1}, more), ({"tp": z - 1}, less)])
+
+        def rows(shard):
+            return pl.ds(pl.multiple_of(shard * own, own), own)
+
+        def copy(way, k, shard):
+            ref = all_ref.at[rows(shard)]
+            return remote(ref, ref, send.at[way, k], recv.at[way, k], {"tp": z + 1 - 2 * way})
+
+        def multiply(shard):
+            block = all_ref[rows(shard), :]
+            at = 0
+            for w_ref, cols in zip(w_refs, parts):
+                y_ref[rows(shard), at:at + cols] = dot_nn(block, w_ref[...])
+                at += cols
+
+        all_ref[rows(z), :] = x_ref[...]
+        pl.when(more)(lambda: copy(0, 0, z).start())
+        pl.when(less)(lambda: copy(1, 0, z).start())
+        multiply(z)
+
+        def step(k, _):
+            from_left, from_right = z - 1 - k, z + 1 + k
+            left, right = from_left >= 0, from_right < n
+
+            @pl.when(left)
+            def _():
+                copy(0, k, from_left).wait_recv()
+                pl.when(more)(lambda: copy(0, k + 1, from_left).start())
+
+            @pl.when(right)
+            def _():
+                copy(1, k, from_right).wait_recv()
+                pl.when(less)(lambda: copy(1, k + 1, from_right).start())
+
+            pl.when(left)(lambda: multiply(from_left))
+            pl.when(right)(lambda: multiply(from_right))
+            return 0
+
+        lax.fori_loop(0, n - 1, step, 0)
+
+        def sent(k, _):
+            pl.when(more & (z - k >= 0))(lambda: copy(0, k, z - k).wait_send())
+            pl.when(less & (z + k < n))(lambda: copy(1, k, z + k).wait_send())
+            return 0
+
+        lax.fori_loop(0, n - 1, sent, 0)
+
+    total = sum(parts)
+    return pl.pallas_call(
+        kernel,
+        out_shape=[jax.ShapeDtypeStruct((n * own, width), x.dtype), jax.ShapeDtypeStruct((n * own, total), f_type)],
+        in_specs=in_vmem(1 + len(weights)), out_specs=in_vmem(2),
+        scratch_shapes=[pltpu.SemaphoreType.DMA((2, n))] * 2,
+        compiler_params=comm_params(collective_id), name="gather_project",
+        cost_estimate=cost(2 * n * own * width * total, 4 * n * own * total, 0))(x, *weights)
+
+
+def project_scatter(grads, weights, n, collective_id):
+    own = grads[0].shape[0] // n
+    width = weights[0].shape[0]
+    m = len(grads)
+
+    def kernel(*refs):
+        g_refs, w_refs = refs[:m], refs[m:2 * m]
+        o_ref, out_buf, in_buf, send, recv = refs[2 * m:]
+        z = lax.axis_index("tp")
+        more, less = z + 1 < n, z > 0
+        meet([({"tp": z + 1}, more), ({"tp": z - 1}, less)])
+
+        def rows(shard):
+            return pl.ds(pl.multiple_of(shard * own, own), own)
+
+        def partial(shard):
+            return sum(dot_nt(g_ref[rows(shard), :], w_ref[...]) for g_ref, w_ref in zip(g_refs, w_refs))
+
+        def copy(way, shard):
+            return remote(out_buf.at[shard], in_buf.at[way, shard], send.at[shard], recv.at[way, shard],
+                          {"tp": z + 1 - 2 * way})
+
+        def step(t, _):
+            right_target, left_target = n - 1 - (t - z), t - (n - 1 - z)
+
+            @pl.when((right_target < n) & (right_target > z))
+            def _():
+                total = partial(right_target)
+
+                @pl.when(less)
+                def _():
+                    copy(0, right_target).wait_recv()
+                    out_buf[right_target] = (total + in_buf[0, right_target].astype(f_type)).astype(bf_type)
+
+                @pl.when(jnp.logical_not(less))
+                def _():
+                    out_buf[right_target] = total.astype(bf_type)
+
+                copy(0, right_target).start()
+
+            @pl.when((left_target >= 0) & (left_target < z))
+            def _():
+                total = partial(left_target)
+
+                @pl.when(more)
+                def _():
+                    copy(1, left_target).wait_recv()
+                    out_buf[left_target] = (total + in_buf[1, left_target].astype(f_type)).astype(bf_type)
+
+                @pl.when(jnp.logical_not(more))
+                def _():
+                    out_buf[left_target] = total.astype(bf_type)
+
+                copy(1, left_target).start()
+
+            return 0
+
+        lax.fori_loop(0, n - 1, step, 0)
+        o_ref[...] = partial(z)
+
+        @pl.when(less)
+        def _():
+            copy(0, z).wait_recv()
+            o_ref[...] += in_buf[0, z].astype(f_type)
+
+        @pl.when(more)
+        def _():
+            copy(1, z).wait_recv()
+            o_ref[...] += in_buf[1, z].astype(f_type)
+
+        def sent(k, _):
+            pl.when(k > z)(lambda: copy(0, k).wait_send())
+            pl.when(k < z)(lambda: copy(1, k).wait_send())
+            return 0
+
+        lax.fori_loop(0, n, sent, 0)
+
+    return pl.pallas_call(
+        kernel, out_shape=jax.ShapeDtypeStruct((own, width), f_type),
+        in_specs=in_vmem(2 * m), out_specs=in_vmem(1)[0],
+        scratch_shapes=[pltpu.VMEM((n, own, width), bf_type), pltpu.VMEM((2, n, own, width), bf_type),
+                        pltpu.SemaphoreType.DMA((n,)), pltpu.SemaphoreType.DMA((2, n))],
+        compiler_params=comm_params(collective_id), name="project_scatter",
+        cost_estimate=cost(2 * n * own * width * sum(w.shape[1] for w in weights), 3 * n * own * width, 0))(*grads, *weights)
+
+
+def small_exchange(arrays, axis, n, collective_id):
+    m = len(arrays)
+
+    def kernel(*refs):
+        x_refs, o_refs, (send, recv) = refs[:m], refs[m:2 * m], refs[2 * m:]
+        me = lax.axis_index(axis)
+        others = [lax.rem(me + d, n) for d in range(1, n)]
+        meet([({axis: o}, None) for o in others])
+        copies = [remote(x_ref.at[o], o_ref.at[me], send.at[i, d], recv.at[i, d], {axis: o})
+                  for i, (x_ref, o_ref) in enumerate(zip(x_refs, o_refs)) for d, o in enumerate(others)]
+        for c in copies:
+            c.start()
+        for x_ref, o_ref in zip(x_refs, o_refs):
+            o_ref[me] = x_ref[me]
+        for c in copies:
+            c.wait()
+
+    return pl.pallas_call(
+        kernel, out_shape=[jax.ShapeDtypeStruct(x.shape, x.dtype) for x in arrays],
+        in_specs=in_vmem(m), out_specs=in_vmem(m),
+        scratch_shapes=[pltpu.SemaphoreType.DMA((m, n - 1))] * 2,
+        compiler_params=comm_params(collective_id), name=f"small_exchange_{axis}_{collective_id}")(*arrays)
+
+
+SIBLING, ALONG_X, ALONG_Y, ACROSS = 1, 2, 4, 6
+
+
+def flip(s, bit):
+    for b in (1, 2, 4):
+        if bit & b:
+            s = s + b - 2 * b * lax.rem(s // b, 2)
+    return s
+
+
+def plane_ffn(x, slices, g_ffn, collective_id):
+    own, width = x.shape
+    tp, hid = slices.shape[0], slices.shape[2]
+    hidden = tp * hid
+    half = own // 2
+    n = 8
+    tiles = width // hid
+
+    def kernel(x_ref, s_ref, g_ref, all_ref, act_ref, gg_ref, gu_ref, wg_ref, wu_ref, wd_ref, load, send, recv):
+        s = lax.axis_index("seq")
+        sib, px, py, diag = (flip(s, b) for b in (SIBLING, ALONG_X, ALONG_Y, ACROSS))
+        loads = []
+        for r in range(tp):
+            to = slice(r * hid, (r + 1) * hid)
+            loads.append(pltpu.make_async_copy(s_ref.at[r, :width], wg_ref.at[:, to], load.at[len(loads)]))
+            loads.append(pltpu.make_async_copy(s_ref.at[r, width:2 * width], wu_ref.at[:, to], load.at[len(loads)]))
+            for t in range(tiles):
+                loads.append(pltpu.make_async_copy(s_ref.at[r, 2 * width + t * hid:2 * width + (t + 1) * hid],
+                                                   wd_ref.at[to, t * hid:(t + 1) * hid], load.at[len(loads)]))
+        for c in loads:
+            c.start()
+        meet([({"seq": d}, None) for d in (sib, px, py)])
+
+        def rows(shard, part=None):
+            if part is None:
+                return pl.ds(pl.multiple_of(shard * own, own), own)
+            return pl.ds(pl.multiple_of(shard * own + part * half, half), half)
+
+        def copy(i, shard, part, to):
+            ref = all_ref.at[rows(shard, part)]
+            return remote(ref, ref, send.at[i], recv.at[i], {"seq": to})
+
+        all_ref[rows(s), :] = x_ref[...]
+        x_a, x_b, y_b, y_a = copy(0, s, 0, px), copy(1, s, 1, px), copy(2, s, 1, py), copy(3, s, 0, py)
+        c_own = copy(4, s, None, sib)
+        for c in (x_a, y_b, x_b, y_a, c_own):
+            c.start()
+        for c in loads:
+            c.wait()
+
+        def work(shard):
+            block = all_ref[rows(shard), :]
+            gate = dot_nn(block, wg_ref[...])
+            up = dot_nn(block, wu_ref[...])
+            g_act = dot_nt(g_ref[rows(shard), :], wd_ref[...])
+            sig = jax.nn.sigmoid(gate)
+            silu = gate * sig
+            act_ref[rows(shard), :] = (silu * up).astype(bf_type)
+            gu_ref[rows(shard), :] = (g_act * silu).astype(bf_type)
+            gg_ref[rows(shard), :] = (g_act * up * sig * (1.0 + gate * (1.0 - sig))).astype(bf_type)
+
+        work(s)
+        c_own.wait_recv()
+        x_a.wait_recv()
+        y_on = copy(5, px, 0, py)
+        y_on.start()
+        y_b.wait_recv()
+        x_on = copy(6, py, 1, px)
+        x_on.start()
+
+        def later(k, _):
+            @pl.when(k == 0)
+            def _():
+                work(sib)
+                x_b.wait_recv()
+                copy(7, px, None, sib).start()
+                y_a.wait_recv()
+                copy(8, py, None, sib).start()
+
+            @pl.when(k == 1)
+            def _():
+                copy(7, px, None, sib).wait_recv()
+                copy(8, py, None, sib).wait_recv()
+
+            @pl.when(k == 2)
+            def _():
+                y_on.wait_recv()
+                x_on.wait_recv()
+                copy(9, diag, None, sib).start()
+
+            @pl.when(k == 3)
+            def _():
+                copy(9, diag, None, sib).wait_recv()
+
+            first = jnp.where(k == 0, px, jnp.where(k == 1, flip(px, SIBLING), jnp.where(k == 2, diag, flip(diag, SIBLING))))
+            work(first)
+
+            @pl.when(k < 2)
+            def _():
+                work(jnp.where(k == 0, py, flip(py, SIBLING)))
+
+            return 0
+
+        lax.fori_loop(0, 4, later, 0)
+        for c in (x_a, x_b, y_b, y_a, c_own, y_on, x_on, copy(7, px, None, sib), copy(8, py, None, sib), copy(9, diag, None, sib)):
+            c.wait_send()
+
+    any_spec = pl.BlockSpec(memory_space=pl.ANY)
+    low = jax.ShapeDtypeStruct((n * own, hidden), bf_type)
+    return pl.pallas_call(
+        kernel, out_shape=[jax.ShapeDtypeStruct((n * own, width), bf_type), low, low, low],
+        in_specs=[in_vmem(1)[0], any_spec, in_vmem(1)[0]], out_specs=in_vmem(4),
+        scratch_shapes=[pltpu.VMEM((width, hidden), bf_type), pltpu.VMEM((width, hidden), bf_type),
+                        pltpu.VMEM((hidden, width), bf_type), pltpu.SemaphoreType.DMA((tp * (2 + tiles),)),
+                        pltpu.SemaphoreType.DMA((10,)), pltpu.SemaphoreType.DMA((10,))],
+        compiler_params=comm_params(collective_id), name="plane_ffn",
+        cost_estimate=cost(6 * n * own * width * hidden, 4 * n * own * width, 0))(x, slices, g_ffn)
+
+
+def plane_sum(partial_of, own, width, s, refs, store):
+    stage, c_in, hop_x, hop_y, in_x, in_y, send, recv = refs
+    half = own // 2
+    sib, px, py, diag = (flip(s, b) for b in (SIBLING, ALONG_X, ALONG_Y, ACROSS))
+    top, bottom = pl.ds(0, half), pl.ds(half, half)
+
+    def to_sibling(i, target):
+        stage[i] = partial_of(flip(target, SIBLING)).astype(bf_type)
+        c = remote(stage.at[i], c_in.at[i], send.at[i], recv.at[i], {"seq": sib})
+        c.start()
+        return c
+
+    def hop(i, src, dst, to):
+        return remote(src, dst, send.at[i], recv.at[i], {"seq": to})
+
+    c_diag = to_sibling(0, diag)
+    mine = partial_of(diag)
+    c_x = to_sibling(1, px)
+    c_diag.wait_recv()
+    stage[4] = (mine + c_in[0].astype(f_type)).astype(bf_type)
+    d_y = hop(4, stage.at[4, top], hop_y, py)
+    d_x = hop(5, stage.at[4, bottom], hop_x, px)
+    d_y.start()
+    d_x.start()
+    mine = partial_of(px)
+    c_y = to_sibling(2, py)
+    c_x.wait_recv()
+    stage[5, half:, :] = (mine[half:] + c_in[1, half:, :].astype(f_type)).astype(bf_type)
+    x_b = hop(6, stage.at[5, bottom], in_x.at[bottom], px)
+    x_b.start()
+    mine_y = partial_of(py)
+    c_own = to_sibling(3, s)
+    c_y.wait_recv()
+    stage[6, :half, :] = (mine_y[:half] + c_in[2, :half, :].astype(f_type)).astype(bf_type)
+    y_a = hop(7, stage.at[6, top], in_y.at[top], py)
+    y_a.start()
+    d_y.wait_recv()
+    stage[5, :half, :] = (mine[:half] + c_in[1, :half, :].astype(f_type) + hop_y[...].astype(f_type)).astype(bf_type)
+    x_a = hop(8, stage.at[5, top], in_x.at[top], px)
+    x_a.start()
+    d_x.wait_recv()
+    stage[6, half:, :] = (mine_y[half:] + c_in[2, half:, :].astype(f_type) + hop_x[...].astype(f_type)).astype(bf_type)
+    y_b = hop(9, stage.at[6, bottom], in_y.at[bottom], py)
+    y_b.start()
+    total = partial_of(s)
+    c_own.wait_recv()
+    total = total + c_in[3].astype(f_type)
+    x_b.wait_recv()
+    y_a.wait_recv()
+    x_a.wait_recv()
+    y_b.wait_recv()
+    store(total + in_x[...].astype(f_type) + in_y[...].astype(f_type))
+    for c in (c_diag, c_x, c_y, c_own, d_y, d_x, x_b, y_a, x_a, y_b):
+        c.wait_send()
+
+
+def plane_sum_scratch(own, width):
+    half = own // 2
+    return [pltpu.VMEM((7, own, width), bf_type), pltpu.VMEM((4, own, width), bf_type),
+            pltpu.VMEM((half, width), bf_type), pltpu.VMEM((half, width), bf_type),
+            pltpu.VMEM((own, width), bf_type), pltpu.VMEM((own, width), bf_type),
+            pltpu.SemaphoreType.DMA((10,)), pltpu.SemaphoreType.DMA((10,))]
+
+
+def plane_project_scatter(gg, gu, slices, collective_id):
+    n = 8
+    own = gg.shape[0] // n
+    tp, hid = slices.shape[0], slices.shape[2]
+    hidden, width = tp * hid, slices.shape[1] // 3
+
+    def kernel(gg_ref, gu_ref, s_ref, o_ref, wg_ref, wu_ref, load, *refs):
+        s = lax.axis_index("seq")
+        loads = []
+        for r in range(tp):
+            to = slice(r * hid, (r + 1) * hid)
+            loads.append(pltpu.make_async_copy(s_ref.at[r, :width], wg_ref.at[:, to], load.at[2 * r]))
+            loads.append(pltpu.make_async_copy(s_ref.at[r, width:2 * width], wu_ref.at[:, to], load.at[2 * r + 1]))
+        for c in loads:
+            c.start()
+        meet([({"seq": flip(s, b)}, None) for b in (SIBLING, ALONG_X, ALONG_Y)])
+        for c in loads:
+            c.wait()
+
+        def partial_of(shard):
+            rows = pl.ds(pl.multiple_of(shard * own, own), own)
+            return dot_nt(gg_ref[rows, :], wg_ref[...]) + dot_nt(gu_ref[rows, :], wu_ref[...])
+
+        def store(total):
+            o_ref[...] = total
+
+        plane_sum(partial_of, own, width, s, refs, store)
+
+    return pl.pallas_call(
+        kernel, out_shape=jax.ShapeDtypeStruct((own, width), f_type),
+        in_specs=in_vmem(2) + [pl.BlockSpec(memory_space=pl.ANY)], out_specs=in_vmem(1)[0],
+        scratch_shapes=[pltpu.VMEM((width, hidden), bf_type), pltpu.VMEM((width, hidden), bf_type),
+                        pltpu.SemaphoreType.DMA((2 * tp,)), *plane_sum_scratch(own, width)],
+        compiler_params=comm_params(collective_id), name="plane_project_scatter",
+        cost_estimate=cost(4 * n * own * width * hidden, 4 * n * own * width, 0))(gg, gu, slices)
+
+
+def plane_gather(view, s, send, recv):
+    sib, px, py, diag = (flip(s, b) for b in (SIBLING, ALONG_X, ALONG_Y, ACROSS))
+
+    def copy(i, shard, part, to):
+        return remote(view(shard, part), view(shard, part), send.at[i], recv.at[i], {"seq": to})
+
+    x_a, x_b, y_b, y_a = copy(0, s, 0, px), copy(1, s, 1, px), copy(2, s, 1, py), copy(3, s, 0, py)
+    c_own, y_on, x_on = copy(4, s, None, sib), copy(5, px, 0, py), copy(6, py, 1, px)
+    c_x, c_y, c_diag = copy(7, px, None, sib), copy(8, py, None, sib), copy(9, diag, None, sib)
+
+    def start():
+        for c in (x_a, y_b, x_b, y_a, c_own):
+            c.start()
+
+    def turn():
+        x_a.wait_recv()
+        y_on.start()
+        y_b.wait_recv()
+        x_on.start()
+
+    def share():
+        x_b.wait_recv()
+        c_x.start()
+        y_a.wait_recv()
+        c_y.start()
+
+    def last():
+        y_on.wait_recv()
+        x_on.wait_recv()
+        c_diag.start()
+
+    def finish():
+        for c in (c_own, c_x, c_y, c_diag):
+            c.wait_recv()
+        for c in (x_a, x_b, y_b, y_a, c_own, y_on, x_on, c_x, c_y, c_diag):
+            c.wait_send()
+
+    return start, turn, share, last, finish
+
+
+def gather_project_both(x, weights, extra, small, collective_id):
+    n = 4
+    own, width = x.shape
+    parts = [w.shape[1] for w in weights]
+
+    def kernel(x_ref, e_ref, t_ref, *refs):
+        w_refs, (all_ref, y_ref, e_all, t_all, send, recv, p_send, p_recv, t_send, t_recv) = refs[:len(weights)], refs[len(weights):]
+        z, s = lax.axis_index("tp"), lax.axis_index("seq")
+        more, less = z + 1 < n, z > 0
+        others = [lax.rem(z + d, n) for d in range(1, n)]
+        meet([({"tp": o}, None) for o in others] + [({"seq": flip(s, b)}, None) for b in (SIBLING, ALONG_X, ALONG_Y)])
+        smalls = [remote(t_ref, t_all.at[z], t_send.at[d], t_recv.at[d], {"tp": o}) for d, o in enumerate(others)]
+
+        def rows(shard):
+            return pl.ds(pl.multiple_of(shard * own, own), own)
+
+        def copy(way, k, shard):
+            ref = all_ref.at[rows(shard)]
+            return remote(ref, ref, send.at[way, k], recv.at[way, k], {"tp": z + 1 - 2 * way})
+
+        def multiply(shard):
+            block = all_ref[rows(shard), :]
+            at = 0
+            for w_ref, cols in zip(w_refs, parts):
+                y_ref[rows(shard), at:at + cols] = dot_nn(block, w_ref[...])
+                at += cols
+
+        all_ref[rows(z), :] = x_ref[...]
+        pl.when(more)(lambda: copy(0, 0, z).start())
+        pl.when(less)(lambda: copy(1, 0, z).start())
+        e_all[rows(s), :] = e_ref[...]
+
+        def view(shard, part):
+            if part is None:
+                return e_all.at[rows(shard)]
+            return e_all.at[pl.ds(pl.multiple_of(shard * own + part * (own // 2), own // 2), own // 2)]
+
+        start, turn, share, last, finish = plane_gather(view, s, p_send, p_recv)
+        start()
+        t_all[z] = t_ref[...]
+        multiply(z)
+        turn()
+
+        def step(k, _):
+            from_left, from_right = z - 1 - k, z + 1 + k
+            left, right = from_left >= 0, from_right < n
+
+            @pl.when(left)
+            def _():
+                copy(0, k, from_left).wait_recv()
+                pl.when(more)(lambda: copy(0, k + 1, from_left).start())
+
+            @pl.when(right)
+            def _():
+                copy(1, k, from_right).wait_recv()
+                pl.when(less)(lambda: copy(1, k + 1, from_right).start())
+
+            pl.when(k == 0)(share)
+
+            @pl.when(k == 1)
+            def _():
+                last()
+                for c in smalls:
+                    c.start()
+
+            pl.when(left)(lambda: multiply(from_left))
+            pl.when(right)(lambda: multiply(from_right))
+            return 0
+
+        lax.fori_loop(0, n - 1, step, 0)
+
+        def sent(k, _):
+            pl.when(more & (z - k >= 0))(lambda: copy(0, k, z - k).wait_send())
+            pl.when(less & (z + k < n))(lambda: copy(1, k, z + k).wait_send())
+            return 0
+
+        lax.fori_loop(0, n - 1, sent, 0)
+        finish()
+        for c in smalls:
+            c.wait()
+
+    total = sum(parts)
+    return pl.pallas_call(
+        kernel,
+        out_shape=[jax.ShapeDtypeStruct((n * own, width), x.dtype), jax.ShapeDtypeStruct((n * own, total), f_type),
+                   jax.ShapeDtypeStruct((8 * own, width), extra.dtype),
+                   jax.ShapeDtypeStruct((n, *small.shape), small.dtype)],
+        in_specs=in_vmem(3 + len(weights)), out_specs=in_vmem(4),
+        scratch_shapes=[pltpu.SemaphoreType.DMA((2, n))] * 2 + [pltpu.SemaphoreType.DMA((10,))] * 2
+        + [pltpu.SemaphoreType.DMA((n - 1,))] * 2,
+        compiler_params=comm_params(collective_id), name="gather_project_both",
+        cost_estimate=cost(2 * n * own * width * total, 4 * n * own * total, 0))(x, extra, small, *weights)
+
+
+def scatter_both(grads, weights, act, slices, collective_id):
+    n = 4
+    own = grads[0].shape[0] // n
+    width = weights[0].shape[0]
+    m = len(grads)
+    tp, hid = slices.shape[0], slices.shape[2]
+    hidden = tp * hid
+    tiles = width // hid
+    half = own // 2
+
+    def kernel(*refs):
+        g_refs, w_refs = refs[:m], refs[m:2 * m]
+        (act_ref, s_ref, o_ref, f_ref, out_buf, in_buf, send, recv, wd_ref, load,
+         stage, c_in, hop_x, hop_y, in_x, in_y, p_send, p_recv, keep) = refs[2 * m:]
+        z, s = lax.axis_index("tp"), lax.axis_index("seq")
+        more, less = z + 1 < n, z > 0
+        loads = []
+        for r in range(tp):
+            for t in range(tiles):
+                loads.append(pltpu.make_async_copy(s_ref.at[r, 2 * width + t * hid:2 * width + (t + 1) * hid],
+                                                   wd_ref.at[r * hid:(r + 1) * hid, t * hid:(t + 1) * hid], load.at[len(loads)]))
+        for c in loads:
+            c.start()
+        meet([({"tp": z + 1}, more), ({"tp": z - 1}, less)]
+             + [({"seq": flip(s, b)}, None) for b in (SIBLING, ALONG_X, ALONG_Y)])
+
+        def rows(shard):
+            return pl.ds(pl.multiple_of(shard * own, own), own)
+
+        def partial(shard):
+            return sum(dot_nt(g_ref[rows(shard), :], w_ref[...]) for g_ref, w_ref in zip(g_refs, w_refs))
+
+        def copy(way, shard):
+            return remote(out_buf.at[shard], in_buf.at[way, shard], send.at[shard], recv.at[way, shard],
+                          {"tp": z + 1 - 2 * way})
+
+        def pass_on(way, target, behind):
+            total = partial(target)
+
+            @pl.when(behind)
+            def _():
+                copy(way, target).wait_recv()
+                out_buf[target] = (total + in_buf[way, target].astype(f_type)).astype(bf_type)
+
+            @pl.when(jnp.logical_not(behind))
+            def _():
+                out_buf[target] = total.astype(bf_type)
+
+            copy(way, target).start()
+
+        sib, px, py, diag = (flip(s, b) for b in (SIBLING, ALONG_X, ALONG_Y, ACROSS))
+        top, bottom = pl.ds(0, half), pl.ds(half, half)
+
+        def share_of(shard):
+            return dot_nn(act_ref[rows(shard), :], wd_ref[...])
+
+        def sibling(i):
+            return remote(stage.at[i], c_in.at[i], p_send.at[i], p_recv.at[i], {"seq": sib})
+
+        def hop(i, src, dst, to):
+            return remote(src, dst, p_send.at[i], p_recv.at[i], {"seq": to})
+
+        d_y, d_x = hop(4, stage.at[4, top], hop_y, py), hop(5, stage.at[4, bottom], hop_x, px)
+        x_b, y_a = hop(6, stage.at[5, bottom], in_x.at[bottom], px), hop(7, stage.at[6, top], in_y.at[top], py)
+        x_a, y_b = hop(8, stage.at[5, top], in_x.at[top], px), hop(9, stage.at[6, bottom], in_y.at[bottom], py)
+
+        def first():
+            for c in loads:
+                c.wait()
+            stage[0] = share_of(flip(diag, SIBLING)).astype(bf_type)
+            sibling(0).start()
+            stage[1] = share_of(flip(px, SIBLING)).astype(bf_type)
+            sibling(1).start()
+            stage[2] = share_of(flip(py, SIBLING)).astype(bf_type)
+            sibling(2).start()
+            stage[3] = share_of(sib).astype(bf_type)
+            sibling(3).start()
+            mine = share_of(diag)
+            sibling(0).wait_recv()
+            stage[4] = (mine + c_in[0].astype(f_type)).astype(bf_type)
+            d_y.start()
+            d_x.start()
+            mine = share_of(px)
+            sibling(1).wait_recv()
+            mine = mine + c_in[1].astype(f_type)
+            stage[5, half:, :] = mine[half:].astype(bf_type)
+            x_b.start()
+            keep[:half, :] = mine[:half]
+            mine = share_of(py)
+            sibling(2).wait_recv()
+            mine = mine + c_in[2].astype(f_type)
+            stage[6, :half, :] = mine[:half].astype(bf_type)
+            y_a.start()
+            keep[half:, :] = mine[half:]
+
+        def second():
+            d_y.wait_recv()
+            stage[5, :half, :] = (keep[:half, :] + hop_y[...].astype(f_type)).astype(bf_type)
+            x_a.start()
+            d_x.wait_recv()
+            stage[6, half:, :] = (keep[half:, :] + hop_x[...].astype(f_type)).astype(bf_type)
+            y_b.start()
+
+        def third():
+            total = share_of(s)
+            sibling(3).wait_recv()
+            for c in (x_b, y_a, x_a, y_b):
+                c.wait_recv()
+            f_ref[...] = total + c_in[3].astype(f_type) + in_x[...].astype(f_type) + in_y[...].astype(f_type)
+
+        def step(t, _):
+            right_target, left_target = n - 1 - (t - z), t - (n - 1 - z)
+            pl.when((right_target < n) & (right_target > z))(lambda: pass_on(0, right_target, less))
+            pl.when((left_target >= 0) & (left_target < z))(lambda: pass_on(1, left_target, more))
+            pl.when(t == 0)(first)
+            pl.when(t == 1)(second)
+            return 0
+
+        lax.fori_loop(0, n - 1, step, 0)
+        third()
+        o_ref[...] = partial(z)
+
+        @pl.when(less)
+        def _():
+            copy(0, z).wait_recv()
+            o_ref[...] += in_buf[0, z].astype(f_type)
+
+        @pl.when(more)
+        def _():
+            copy(1, z).wait_recv()
+            o_ref[...] += in_buf[1, z].astype(f_type)
+
+        def sent(k, _):
+            pl.when(k > z)(lambda: copy(0, k).wait_send())
+            pl.when(k < z)(lambda: copy(1, k).wait_send())
+            return 0
+
+        lax.fori_loop(0, n, sent, 0)
+        for i in range(4):
+            sibling(i).wait_send()
+        for c in (d_y, d_x, x_b, y_a, x_a, y_b):
+            c.wait_send()
+
+    one = jax.ShapeDtypeStruct((own, width), f_type)
+    return pl.pallas_call(
+        kernel, out_shape=[one, one],
+        in_specs=in_vmem(2 * m + 1) + [pl.BlockSpec(memory_space=pl.ANY)], out_specs=in_vmem(2),
+        scratch_shapes=[pltpu.VMEM((n, own, width), bf_type), pltpu.VMEM((2, n, own, width), bf_type),
+                        pltpu.SemaphoreType.DMA((n,)), pltpu.SemaphoreType.DMA((2, n)),
+                        pltpu.VMEM((hidden, width), bf_type), pltpu.SemaphoreType.DMA((tp * tiles,)),
+                        *plane_sum_scratch(own, width), pltpu.VMEM((own, width), f_type)],
+        compiler_params=comm_params(collective_id), name="scatter_both",
+        cost_estimate=cost(2 * n * own * width * sum(w.shape[1] for w in weights), 3 * n * own * width, 0))(
+            *grads, *weights, act, slices)
+
+
+def exchange_project(mixed, out_rows, collective_id):
+    n = 4
+    own, inner = mixed.shape[0] // n, mixed.shape[1]
+    cut, width = out_rows.shape[1:]
+
+    def kernel(m_ref, w_ref, y_ref, own_ref, w_all, got, send, recv, p_send, p_recv):
+        z, s = lax.axis_index("tp"), lax.axis_index("seq")
+        others = [lax.rem(z + d, n) for d in range(1, n)]
+        meet([({"tp": o}, None) for o in others] + [({"seq": flip(s, b)}, None) for b in (SIBLING, ALONG_X, ALONG_Y)])
+
+        def rows(shard):
+            return pl.ds(pl.multiple_of(shard * own, own), own)
+
+        copies = [remote(m_ref.at[rows(o)], got.at[z], send.at[d], recv.at[d], {"tp": o}) for d, o in enumerate(others)]
+        for c in copies:
+            c.start()
+        for t in range(n):
+            w_all[t, s] = w_ref[t]
+
+        def view(shard, part):
+            if part is None:
+                return w_all.at[:, shard]
+            return w_all.at[part * (n // 2):(part + 1) * (n // 2), shard]
+
+        start, turn, share, last, finish = plane_gather(view, s, p_send, p_recv)
+        start()
+        got[z] = m_ref[rows(z), :]
+        turn()
+        share()
+        last()
+        for c in copies:
+            c.wait()
+        finish()
+        for t in range(n):
+            own_ref[:, t * inner:(t + 1) * inner] = got[t]
+            part = dot_nn(got[t], w_all[t].reshape(8 * cut, width))
+            if t == 0:
+                y_ref[...] = part
+            else:
+                y_ref[...] += part
+
+    return pl.pallas_call(
+        kernel,
+        out_shape=[jax.ShapeDtypeStruct((own, width), f_type), jax.ShapeDtypeStruct((own, n * inner), bf_type),
+                   jax.ShapeDtypeStruct((n, 8, cut, width), bf_type)],
+        in_specs=in_vmem(2), out_specs=in_vmem(3),
+        scratch_shapes=[pltpu.VMEM((n, own, inner), bf_type)] + [pltpu.SemaphoreType.DMA((n - 1,))] * 2
+        + [pltpu.SemaphoreType.DMA((10,))] * 2,
+        compiler_params=comm_params(collective_id), name="exchange_project",
+        cost_estimate=cost(2 * own * width * width, 10 * own * width, 0))(mixed, out_rows)
 
 
 def rms_parts(values):
@@ -427,9 +1220,14 @@
     own_row = me_tp * own + jnp.arange(own, dtype=jnp.int32)
     own_member = ((own_row[:, None] >= starts[None, :]) & (own_row[:, None] < ends[None, :])).astype(f_type)
 
+    cap_cut = caption.shape[1] // 2
+    caption_a, cond_embed = lax.optimization_barrier((caption[:, :cap_cut], cond_embed))
     silu_cond = jax.nn.silu(cond_embed.astype(f_type)).astype(bf_type)
     mod_local = jnp.einsum("ck,kjd->cjd", silu_cond, ada_weight, preferred_element_type=f_type) + ada_bias.astype(f_type)[None]
-    modulation = lax.all_gather(mod_local, "tp", axis=2, tiled=True)
+    mod_rows, = small_gather([jnp.pad(mod_local.reshape(clips * 6, -1), ((0, -(clips * 6) % 8), (0, 0)))], "tp", tp, 1)
+    cut = out_proj.shape[0] // seq
+    out_slice = lax.dynamic_slice_in_dim(out_proj, me_seq * cut, cut, 0)
+    modulation = mod_rows.transpose(1, 0, 2).reshape(-1, width)[:clips * 6].reshape(clips, 6, width)
 
     def token_mod(which):
         return sum(own_member[:, c:c + 1] * modulation[c, which][None, :] for c in range(clips))
@@ -437,92 +1235,126 @@
     rows_in = tokens.astype(f_type)
     normed_own, factor_own = rms_parts(rows_in)
     modin_own = (normed_own * (1.0 + token_mod(1)) + token_mod(0)).astype(bf_type)
-    modin = lax.all_gather(modin_own, "tp", axis=0, tiled=True)
-    text_all = lax.all_gather(caption, "tp", axis=0, tiled=True)
-
+    grad_y = cotangent.astype(f_type)
+    g_ffn_own = (token_mod(5) * grad_y).astype(bf_type)
     hid = gate_proj.shape[1] // seq
+    planar = seq == 8 and tp == 4 and hid % LANES == 0 and inner % LANES == 0
+    qkv_weights = [pad_lanes(w, wide) for w in (query_proj, key_proj, value_proj)]
+    text_a = lax.all_gather(caption_a, "tp", axis=0, tiled=True)
+    if planar:
+        modin, qkv, g_ffn, out_rows = gather_project_both(modin_own, qkv_weights, g_ffn_own, out_slice, 2)
+    else:
+        modin, qkv = gather_project(modin_own, qkv_weights, tp, 2)
+        g_ffn = lax.all_gather(g_ffn_own, "seq", axis=0, tiled=True)
+        w_out = lax.all_gather(lax.all_gather(out_slice, "tp"), "seq", axis=1).reshape(width, width)
+    caption_b, qkv = lax.optimization_barrier((caption[:, cap_cut:], qkv))
+    text_b = lax.all_gather(caption_b, "tp", axis=0, tiled=True)
+
     gate_slice = lax.dynamic_slice_in_dim(gate_proj, me_seq * hid, hid, 1)
     up_slice = lax.dynamic_slice_in_dim(up_proj, me_seq * hid, hid, 1)
     down_slice = lax.dynamic_slice_in_dim(down_proj, me_seq * hid, hid, 0)
-    w_gate = lax.all_gather(gate_slice, "tp", axis=1, tiled=True)
-    w_up = lax.all_gather(up_slice, "tp", axis=1, tiled=True)
-    w_down = lax.all_gather(down_slice, "tp", axis=0, tiled=True)
-    cut = width // seq
-    out_slice = lax.dynamic_slice_in_dim(out_proj, me_seq * cut, cut, 1)
-    w_out = lax.all_gather(lax.all_gather(out_slice, "tp", axis=0, tiled=True), "seq", axis=1, tiled=True)
-
-    grad_y = cotangent.astype(f_type)
-    g_ffn = lax.all_gather((token_mod(5) * grad_y).astype(bf_type), "seq", axis=0, tiled=True)
-
-    qkv_weight = jnp.concatenate([pad_lanes(query_proj, wide), pad_lanes(key_proj, wide), pad_lanes(value_proj, wide)], axis=1)
-    tkv_weight = jnp.concatenate([pad_lanes(key_text, wide), pad_lanes(value_text, wide)], axis=1)
-    qkv = jnp.dot(modin, qkv_weight, preferred_element_type=f_type)
+    down_turned = down_slice.reshape(hid, -1, hid).transpose(1, 0, 2).reshape(width, hid)
+    slices, text_b = lax.optimization_barrier((jnp.concatenate([gate_slice, up_slice, down_turned], axis=0), text_b))
+    slices = lax.all_gather(slices, "tp", axis=0, tiled=False)
+    w_gate = slices[:, :width].transpose(1, 0, 2).reshape(width, tp * hid)
+    w_up = slices[:, width:2 * width].transpose(1, 0, 2).reshape(width, tp * hid)
+    w_down = slices[:, 2 * width:].reshape(tp, -1, hid, hid).transpose(0, 2, 1, 3).reshape(tp * hid, width)
     qg, kg, tg = (lane_rows(g, pairs) for g in (query_gain, key_gain, text_gain))
     tgate = jnp.tanh(text_gate.astype(f_type))
     gate_rows = lane_rows(jnp.broadcast_to(tgate[:, None], (heads, HEAD)), pairs)
     qrot, krot, self_out, inv = self_attention(lo, hi, qkv, cos, sin, qg, kg, qmask, kmask)
-    tkv = jnp.dot(text_all, tkv_weight, preferred_element_type=f_type)
+    text_weight = jnp.concatenate([pad_lanes(key_text, wide), pad_lanes(value_text, wide)], axis=1)
+    tkv = dot_nn(text_a, text_weight[:cap_cut]) + dot_nn(text_b, text_weight[cap_cut:])
     mixed, cross_out, cinv = cross_attention(clo, chi, qrot, tkv, tg, qmask, tmask, gate_rows, self_out, per_clip)
 
-    mixed_own = lax.all_to_all(mixed[:, :inner], "tp", split_axis=0, concat_axis=1, tiled=True)
-    attn_own = jnp.dot(mixed_own, w_out, preferred_element_type=f_type)
+    if planar:
+        attn_own, mixed_own, w_out = exchange_project(mixed, out_rows, 6)
+        w_out = w_out.reshape(width, width)
+    else:
+        mixed_own = lax.all_to_all(mixed[:, :inner], "tp", split_axis=0, concat_axis=1, tiled=True)
+        attn_own = jnp.dot(mixed_own, w_out, preferred_element_type=f_type)
     hidden_own = rows_in + token_mod(2) * attn_own
     normed_mid, factor_mid = rms_parts(hidden_own)
-    ffn_in = lax.all_gather((normed_mid * (1.0 + token_mod(4)) + token_mod(3)).astype(bf_type), "seq", axis=0, tiled=True)
-    gate_pre = jnp.dot(ffn_in, w_gate, preferred_element_type=f_type)
-    up_pre = jnp.dot(ffn_in, w_up, preferred_element_type=f_type)
-    gate_sig = jax.nn.sigmoid(gate_pre)
-    gate_silu = gate_pre * gate_sig
-    act = (gate_silu * up_pre).astype(bf_type)
-    g_act = dot_nt(g_ffn, w_down)
-    g_up = (g_act * gate_silu).astype(bf_type)
-    g_gate = (g_act * up_pre * gate_sig * (1.0 + gate_pre * (1.0 - gate_sig))).astype(bf_type)
-    g_mid = lax.psum_scatter((dot_nt(g_gate, w_gate) + dot_nt(g_up, w_up)).astype(bf_type), "seq", scatter_dimension=0, tiled=True).astype(f_type)
-    ffn_own = lax.psum_scatter(jnp.dot(act, w_down, preferred_element_type=f_type).astype(bf_type), "seq", scatter_dimension=0, tiled=True).astype(f_type)
-    output = (hidden_own + token_mod(5) * ffn_own).astype(bf_type)
-
-    d_gate = lax.psum_scatter(dot_tn(ffn_in, g_gate).astype(bf_type), "tp", scatter_dimension=1, tiled=True)
-    d_up = lax.psum_scatter(dot_tn(ffn_in, g_up).astype(bf_type), "tp", scatter_dimension=1, tiled=True)
-    d_down = lax.psum_scatter(dot_tn(act, g_ffn).astype(bf_type), "tp", scatter_dimension=0, tiled=True)
-    d_gate = lax.all_to_all(d_gate, "seq", split_axis=0, concat_axis=1, tiled=True).astype(f_type)
-    d_up = lax.all_to_all(d_up, "seq", split_axis=0, concat_axis=1, tiled=True).astype(f_type)
-    d_down = lax.all_to_all(d_down, "seq", split_axis=1, concat_axis=0, tiled=True).astype(f_type)
+    ffn_own_in = (normed_mid * (1.0 + token_mod(4)) + token_mod(3)).astype(bf_type)
+    if planar:
+        ffn_in, act, g_gate, g_up = plane_ffn(ffn_own_in, slices, g_ffn, 4)
+        g_mid = plane_project_scatter(g_gate, g_up, slices, 5)
+    else:
+        ffn_in = lax.all_gather(ffn_own_in, "seq", axis=0, tiled=True)
+        gate_pre = jnp.dot(ffn_in, w_gate, preferred_element_type=f_type)
+        up_pre = jnp.dot(ffn_in, w_up, preferred_element_type=f_type)
+        gate_sig = jax.nn.sigmoid(gate_pre)
+        gate_silu = gate_pre * gate_sig
+        act = (gate_silu * up_pre).astype(bf_type)
+        g_act = dot_nt(g_ffn, w_down)
+        g_up = (g_act * gate_silu).astype(bf_type)
+        g_gate = (g_act * up_pre * gate_sig * (1.0 + gate_pre * (1.0 - gate_sig))).astype(bf_type)
+        g_mid = lax.psum_scatter((dot_nt(g_gate, w_gate) + dot_nt(g_up, w_up)).astype(bf_type), "seq", scatter_dimension=0, tiled=True).astype(f_type)
 
     g_hidden = grad_y + rms_back(g_mid * (1.0 + token_mod(4)), normed_mid, factor_mid)
     g_attn = (token_mod(2) * g_hidden).astype(bf_type)
     d_out = lax.psum_scatter(dot_tn(mixed_own, g_attn).astype(bf_type), "seq", scatter_dimension=1, tiled=True)
-    d_out = lax.psum_scatter(d_out, "tp", scatter_dimension=0, tiled=True).astype(f_type)
     g_mixed = lax.all_to_all(dot_nt(g_attn, w_out).astype(bf_type), "tp", split_axis=1, concat_axis=0, tiled=True)
+
+    d_ffn = jnp.concatenate([dot_tn(g, x).astype(bf_type).reshape(tp, hid, width)
+                             for g, x in ((g_gate, ffn_in), (g_up, ffn_in), (act, g_ffn))], axis=1)
+    d_ffn, g_mixed = lax.optimization_barrier((d_ffn, g_mixed))
+    d_ffn = lax.psum_scatter(d_ffn, "tp", scatter_dimension=0, tiled=False)
+    d_ffn = lax.all_to_all(d_ffn.reshape(3 * hid, seq, width // seq), "seq", split_axis=1, concat_axis=0, tiled=False)
+    d_ffn = d_ffn.reshape(seq, 3, hid, width // seq).astype(f_type)
+    d_gate, d_up = (d_ffn[:, i].reshape(seq * hid, width // seq).T for i in range(2))
+    d_down = d_ffn[:, 2].reshape(seq * hid, width // seq)
 
     gq, gk, gv, gtk, gtv, dqg, dkg, dtg, dgate = attention_back(
         lo, hi, clo, chi, qrot, krot, qkv, tkv, self_out, inv, cross_out, cinv, pad_lanes(g_mixed, wide), gate_rows,
         cos, sin, qg, kg, tg, qmask, kmask, tmask, per_clip, scale)
     gq, gk, gv, gtk, gtv = (g[:, :inner] for g in (gq, gk, gv, gtk, gtv))
-    g_modin = lax.psum_scatter((dot_nt(gq, query_proj) + dot_nt(gk, key_proj) + dot_nt(gv, value_proj)).astype(bf_type),
-                               "tp", scatter_dimension=0, tiled=True).astype(f_type)
-
-    def over_seq(grad):
-        return lax.psum_scatter(grad.astype(bf_type), "seq", scatter_dimension=0, tiled=True).astype(f_type)
-
-    d_query, d_key, d_value = (over_seq(dot_tn(modin, g)) for g in (gq, gk, gv))
-    d_ktext, d_vtext = (over_seq(dot_tn(text_all, g)) for g in (gtk, gtv))
+
+    grads = [dot_tn(modin, g).astype(bf_type) for g in (gq, gk, gv)] + [
+        jnp.concatenate([dot_tn(text_a, g), dot_tn(text_b, g)], axis=0).astype(bf_type) for g in (gtk, gtv)]
+    merged, gq = lax.optimization_barrier((jnp.concatenate([g.reshape(seq, -1, inner) for g in grads], axis=1), gq))
+    merged = lax.psum_scatter(merged, "seq", scatter_dimension=0, tiled=False)
+    proj = [query_proj, key_proj, value_proj]
+    if planar:
+        g_modin, ffn_own = scatter_both([gq, gk, gv], proj, act, slices, 3)
+    else:
+        g_modin = project_scatter([gq, gk, gv], proj, tp, 3)
+        ffn_own = lax.psum_scatter(dot_nn(act, w_down).astype(bf_type), "seq", scatter_dimension=0, tiled=True).astype(f_type)
+    output = (hidden_own + token_mod(5) * ffn_own).astype(bf_type)
+    rows_q, rows_t = width // seq, caption.shape[1] // seq
+    d_query, d_key, d_value = (merged[i * rows_q:(i + 1) * rows_q].astype(f_type) for i in range(3))
+    d_ktext, d_vtext = (merged[3 * rows_q + i * rows_t:3 * rows_q + (i + 1) * rows_t].astype(f_type) for i in range(2))
     grad_tokens = (g_hidden + rms_back(g_modin * (1.0 + token_mod(1)), normed_own, factor_own)).astype(bf_type)
 
     pieces = (g_modin, g_modin * normed_own, g_hidden * attn_own, g_mid, g_mid * normed_mid, grad_y * ffn_own)
     clip_grad = jnp.stack([jnp.stack([jnp.sum(own_member[:, c:c + 1] * p, axis=0) for p in pieces]) for c in range(clips)])
-    g_mod = lax.psum_scatter(clip_grad, "tp", scatter_dimension=2, tiled=True)
-    every_mod = lax.all_gather(g_mod, "seq", axis=0, tiled=True)
-    every_cond = lax.all_gather(silu_cond, "seq", axis=0, tiled=True)
+    mod_parts = clip_grad.reshape(clips * 6, tp, width // tp).transpose(1, 0, 2)
+    mod_parts = jnp.pad(mod_parts, ((0, 0), (0, -(clips * 6) % 8), (0, 0)))
+    if planar:
+        mod_parts, d_out = small_exchange([mod_parts, d_out.reshape(tp, -1, d_out.shape[1])], "tp", tp, 7)
+        d_out = jnp.sum(d_out.astype(f_type), axis=0)
+    else:
+        mod_parts, = small_exchange([mod_parts], "tp", tp, 7)
+        d_out = lax.psum_scatter(d_out, "tp", scatter_dimension=0, tiled=True).astype(f_type)
+    g_mod = jnp.sum(mod_parts, axis=0)
+
+    def gains(d):
+        return d.reshape(-1)[:inner].reshape(heads, HEAD)
+
+    row_gate = jnp.sum(gains(dgate), axis=1) * (1.0 - tgate * tgate)
+    small = jnp.concatenate([dqg[:, 0], dkg[:, 0], dtg[:, 0], pad_lanes(row_gate[None], LANES)], axis=0)
+    small = jnp.pad(small, ((0, -small.shape[0] % 8), (0, 0)))
+    cond_rows = jnp.pad(silu_cond, ((0, 16 - clips), (0, 0)))
+    every_mod, every_small, every_cond = small_gather([g_mod, small, cond_rows], "seq", seq, 8)
+    every_mod = every_mod[:, :clips * 6].reshape(seq * clips, 6, -1)
+    every_cond = every_cond[:, :clips].reshape(seq * clips, -1)
     span = every_cond.shape[1] // seq
     my_cond = lax.dynamic_slice_in_dim(every_cond, me_seq * span, span, 1).astype(f_type)
     d_adaw = jnp.einsum("ck,cjd->kjd", my_cond, every_mod, precision=lax.Precision.HIGHEST)
     d_adab = jnp.sum(every_mod, axis=0)
-
-    def gains(d):
-        return d.reshape(-1)[:inner].reshape(heads, HEAD)
-
-    d_tgate = jnp.sum(gains(dgate), axis=1) * (1.0 - tgate * tgate)
-    d_qgain, d_kgain, d_tgain, d_tgate = lax.psum((gains(dqg), gains(dkg), gains(dtg), d_tgate), "seq")
+    small = jnp.sum(every_small, axis=0)
+    d_qgain, d_kgain, d_tgain = (gains(small[i * pairs:(i + 1) * pairs]) for i in range(3))
+    d_tgate = small[3 * pairs, :heads]
     return (output, grad_tokens, d_query, d_key, d_value, d_out, d_gate, d_up, d_down, d_ktext, d_vtext, d_adaw,
             d_adab, d_qgain, d_kgain, d_tgain, d_tgate)
 

time: 1310 us -> 882 us (0.67)
  waiting for transfers between devices: 720 us -> 96.8 us
  Pallas kernels: 139 us -> 557 us
  matrix products: 195 us -> 78.1 us
  blocking collectives: 80 us -> 0 us
  starting transfers between devices: 38.4 us -> 8.89 us
    pallas_call x0 -> x8, Pallas kernels: none -> 417 us  [the longest x1 107 us: scatter_both(): pl.pallas_call(kernel, out_shape=[one, one], in_specs=in_vmem(2 * m + 1)...]
    reduce_scatter x9 -> x2, waiting for transfers between devices: 315 us -> 0.01 us  [the longest x1 0.01 us: body(): d_ffn = lax.psum_scatter(d_ffn, 'tp', scatter_dimension=0, tiled=False)]
    all_gather x8 -> x3, waiting for transfers between devices: 292 us -> 85.3 us  [the longest x1 56.7 us: body(): text_b = lax.all_gather(caption_b, 'tp', axis=0, tiled=True)]
    dot_general x7 -> x1, matrix products: 60.2 us -> 2.18 us  [dot_nt(): lax.dot_general(a, b, (((1,), (1,)), ((), ())), preferred_element_type=f_...]
    all_gather x4 -> x0, blocking collectives: 56.7 us -> none  [the longest x1 20.4 us: body(): lax.all_gather(out_slice, 'tp', axis=0, tiled=True)]
    all_to_all x4 -> x1, waiting for transfers between devices: 52.7 us -> 0.01 us  [body(): lax.all_to_all(d_ffn.reshape(3 * hid, seq, width // seq), 'seq', split_ax...]
    dot_general x6 -> x2, matrix products: 58.9 us -> 11.7 us  [dot_nn(): return jnp.dot(a, b, preferred_element_type=f_type)]
    unnamed x26 -> x6, waiting for transfers between devices: 45 us -> 0.78 us
  transfers between devices with their start and end apart: 27 -> 8, of which waited for: 18 -> 4; matrix products, arithmetic and copies ran while one was open for 17% -> 15% of each run, Pallas kernels for 11% -> 39%
where the time goes in v2:
time: 882 us; the launch traced here: 874 us
  Pallas kernels  557 us (63%)
  waiting for transfers between devices  96.8 us (11%)
  matrix products  78.1 us (9%)
  other arithmetic  63 us (7%)
  local copies, waits for them, and re-layouts  54.7 us (6%)
  between operations  15.6 us (2%)
  starting transfers between devices  8.89 us (1%)
    pallas_call x1, Pallas kernels, scatter_both(): pl.pallas_call(kernel, out_shape=[one, one], in_specs=in_vmem(2 * m + 1)...  107 us
    pallas_call x1, Pallas kernels, gather_project_both(): pl.pallas_call(kernel, out_shape=[jax.ShapeDtypeStruct((n * own, width),...  99.3 us
    pallas_call x1, Pallas kernels, attention_back(): pl.pallas_call(functools.partial(back_kernel, per_clip=per_clip, scale=sc...  80.2 us
    dot_general x11, matrix products, dot_tn(): lax.dot_general(a, b, (((0,), (0,)), ((), ())), preferred_element_type=f_...  59.5 us
    pallas_call x1, Pallas kernels, plane_ffn(): pl.pallas_call(kernel, out_shape=[jax.ShapeDtypeStruct((n * own, width),...  57 us
    all_gather x1, waiting for transfers between devices, body(): text_b = lax.all_gather(caption_b, 'tp', axis=0, tiled=True)  56.7 us
    pallas_call x1, Pallas kernels, exchange_project(): pl.pallas_call(kernel, out_shape=[jax.ShapeDtypeStruct((own, width), f_ty...  56.2 us
    pallas_call x1, Pallas kernels, plane_project_scatter(): pl.pallas_call(kernel, out_shape=jax.ShapeDtypeStruct((own, width), f_typ...  51.5 us
  transfers between devices with their start and end apart: 8, of which 4 were waited for; matrix products, arithmetic and copies ran while one was open for 15% of the time, Pallas kernels for 39%

profile of v2, /device:TPU:0, one launch (start us, length us, event | category | flops | bytes accessed | tf_op | source)
XLA Modules:
  0.0 874.2 jit_solution(6478895842174665656)
XLA Ops:
  11.3 2.7 fusion.45
  14.0 3.1 convolution_add_fusion
  17.7 10.1 %small_gather_tp_1.1 = f32[4,24,384]{2,1,0:T(8,128)} custom-call(f32[24,384]{1,0:T(8,128)} %pad.20.refs_0_), custom_call_target="tpu_custom_call" | custom-call | tf_op jit(solution)/shard_map/small_gather_tp_1/pallas_call | solution.py:408
  31.4 4.3 fusion.16
  35.8 99.3 %gather_project_both.1 = (bf16[1536,1536]{1,0:T(8,128)(2,1)}, f32[1536,1152]{1,0:T(8,128)}, bf16[3072,1536]{1,0:T(8,128)(2,1)}, bf16[4,48,1536]{2,1,0:T(8,128)(2,1)}) custom-call(bf16[384,1536]{1,0:T(8,128)(2,1)} %get-tuple-element.237.x_ref, bf16[384,1536]{1,0:T(8,128)(2,1)} %get-tuple-element.236.e_ref, ...), custom_call_target="tpu_custom_call" | custom-call | flops 5435817984 | bytes 7077888 | tf_op jit(solution)/shard_map/gather_project_both/pallas_call | solution.py:933
  143.1 56.7 %all-gather.7.cloned.1.call-done = bf16[768,2048]{1,0:T(8,128)(2,1)} async-done(((bf16[192,2048]{1,0:T(8,128)(2,1)}), bf16[768,2048]{1,0:T(8,128)(2,1)}) %all-gather.7.cloned.1.call-update) | async-done | bytes 3145744 | tf_op jit(solution)/shard_map/all_gather | solution.py:1251
  202.3 2.8 fusion.25
  205.1 2.4 pad_maximum_fusion.4
  208.7 42.0 %self_attention.1 = (bf16[1536,384]{1,0:T(8,128)(2,1)}, bf16[1536,384]{1,0:T(8,128)(2,1)}, f32[1536,384]{1,0:T(8,128)}, f32[1536,384]{1,0:T(8,128)}) custom-call(s32[6]{0:T(128)} %get-tuple-element.239.lo, s32[6]{0:T(128)} %get-tuple-element.238.hi, f32[1536,1152]{1,0:T(8,128)} %get-tuple-element.63.q_ref.k_ref.v_ref, ...), custom_call_target="tpu_custom_call" | custom-call | flops 3623878656 | bytes 14155776 | tf_op jit(solution)/shard_map/self_attention/pallas_call | solution.py:300
  253.2 2.7 copy-done.11
  255.9 4.1 fusion.4
  260.0 4.2 all-gather.5.cloned.1.call-done
  264.2 7.6 fusion.19.tk_ref.tv_ref
  271.8 17.5 %cross_attention.1 = (bf16[1536,384]{1,0:T(8,128)(2,1)}, f32[1536,384]{1,0:T(8,128)}, f32[1536,384]{1,0:T(8,128)}) custom-call(s32[6]{0:T(128)} %copy-done.43, s32[6]{0:T(128)} %broadcast_add_fusion.chi, bf16[1536,384]{1,0:T(8,128)(2,1)} %get-tuple-element.64.qrot_ref, f32[768,768]{1,0:T(8,128)} %fusion.19.tk_ref.tv_ref, f32[768,768]{1,0:T(8,128)} %fusion.19.tk_ref.tv_ref, ...), custom_call_target="tpu_custom_call" | custom-call | flops 1207959552 | bytes 8257536 | tf_op jit(solution)/shard_map/cross_attention/pallas_call | solution.py:320
  289.4 56.2 %exchange_project.1 = (f32[384,1536]{1,0:T(8,128)}, bf16[384,1536]{1,0:T(8,128)(2,1)}, bf16[4,8,48,1536]{3,2,1,0:T(8,128)(2,1)}) custom-call(bf16[1536,384]{1,0:T(8,128)(2,1)} %get-tuple-element.69.m_ref, bf16[4,48,1536]{2,1,0:T(8,128)(2,1)} %get-tuple-element.70.w_ref), custom_call_target="tpu_custom_call" | custom-call | flops 1811939328 | bytes 5898240 | tf_op jit(solution)/shard_map/exchange_project/pallas_call | solution.py:1142
  345.7 2.6 multiply_reduce_fusion.19
  348.4 6.0 add_convert_fusion.1.x_ref
  354.4 24.5 %all-gather.9.cloned.1.call-done = bf16[18432,128]{1,0:T(8,128)(2,1)} async-done(((bf16[4608,128]{1,0:T(8,128)(2,1)}), bf16[18432,128]{1,0:T(8,128)(2,1)}) %all-gather.9.cloned.1.call-update) | async-done | bytes 4718608 | tf_op jit(solution)/shard_map/all_gather | solution.py:1258
  378.8 57.0 %plane_ffn.1 = (bf16[3072,1536]{1,0:T(8,128)(2,1)}, bf16[3072,512]{1,0:T(8,128)(2,1)}, bf16[3072,512]{1,0:T(8,128)(2,1)}, bf16[3072,512]{1,0:T(8,128)(2,1)}) custom-call(bf16[384,1536]{1,0:T(8,128)(2,1)} %add_convert_fusion.1.x_ref, bf16[4,4608,128]{2,1,0:T(8,128)(2,1)} %bitcast.179, bf16[3072,1536]{1,0:T(8,128)(2,1)} %get-tuple-element.78.g_ref), custom_call_target="tpu_custom_call" | custom-call | flops 14495514624 | bytes 18874368 | tf_op jit(solution)/shard_map/plane_ffn/pallas_call | solution.py:700
  435.8 10.3 %convolution_convert_fusion.1 = bf16[512,1536]{1,0:T(8,128)(2,1)} fusion(bf16[3072,512]{1,0:T(8,128)(2,1)} %get-tuple-element.82.refs_6_, bf16[3072,1536]{1,0:T(8,128)(2,1)} %get-tuple-element.78.g_ref), kind=kOutput, calls=%fused_computation.18 | convolution fusion | flops 4832624640 | bytes 14155776 | tf_op jit(solution)/shard_map/dot_general | solution.py:27
  446.1 2.6 copy.106
  448.7 10.4 %convolution_convert_fusion.2 = bf16[512,1536]{1,0:T(8,128)(2,1)} fusion(bf16[3072,512]{1,0:T(8,128)(2,1)} %get-tuple-element.81.gu_ref, bf16[3072,1536]{1,0:T(8,128)(2,1)} %get-tuple-element.80), kind=kOutput, calls=%fused_computation.19 | convolution fusion | flops 4832624640 | bytes 14155776 | tf_op jit(solution)/shard_map/dot_general | solution.py:27
  459.2 51.5 %plane_project_scatter.1 = f32[384,1536]{1,0:T(8,128)} custom-call(bf16[3072,512]{1,0:T(8,128)(2,1)} %get-tuple-element.79.gg_ref, bf16[3072,512]{1,0:T(8,128)(2,1)} %get-tuple-element.81.gu_ref, bf16[4,4608,128]{2,1,0:T(8,128)(2,1)} %bitcast.180), custom_call_target="tpu_custom_call" | custom-call | flops 9663676416 | bytes 18874368 | tf_op jit(solution)/shard_map/plane_project_scatter/pallas_call | solution.py:802
  510.7 2.8 copy.105
  513.5 4.8 multiply_reduce_fusion.14
  519.6 2.2 convolution_convert_fusion.7
  522.9 4.3 all-to-all-start
  527.2 10.3 %convolution_convert_fusion.3 = bf16[512,1536]{1,0:T(8,128)(2,1)} fusion(bf16[3072,512]{1,0:T(8,128)(2,1)} %get-tuple-element.79.gg_ref, bf16[3072,1536]{1,0:T(8,128)(2,1)} %get-tuple-element.80), kind=kOutput, calls=%fused_computation.20 | convolution fusion | flops 4832624640 | bytes 14155776 | tf_op jit(solution)/shard_map/dot_general | solution.py:27
  537.5 2.6 copy.104
  540.1 5.2 pad_maximum_fusion
  545.3 10.7 %all-to-all-done = bf16[384,4,384]{2,0,1:T(8,128)(2,1)} async-done(((bf16[384,4,384]{2,0,1:T(8,128)(2,1)}), bf16[384,4,384]{2,0,1:T(8,128)(2,1)}, u32[]{:S(2)}, u32[]{:S(2)}) %all-to-all-start) | async-done | bytes 1179680 | tf_op jit(solution)/shard_map/all_to_all | solution.py:1297
  556.1 7.0 convolution_convert_fusion
  563.2 80.2 %attention_back.1 = (bf16[1536,384]{1,0:T(8,128)(2,1)}, bf16[1536,384]{1,0:T(8,128)(2,1)}, bf16[1536,384]{1,0:T(8,128)(2,1)}, bf16[768,384]{1,0:T(8,128)(2,1)}, ...) custom-call(s32[6]{0:T(128)} %get-tuple-element.239.lo, ...), custom_call_target="tpu_custom_call" | custom-call | flops 9059696640 | bytes 21233664 | tf_op jit(solution)/shard_map/attention_back/pallas_call | solution.py:351
  643.4 5.5 convolution_convert_fusion.6
  650.6 5.6 convolution_convert_fusion.5
  658.0 2.6 convolution_convert_fusion.4
  667.9 2.1 convolution_convert_fusion.8
  672.2 2.0 constant_dynamic-update-slice_fusion.2
  676.6 107.1 %scatter_both.1 = (f32[384,1536]{1,0:T(8,128)}, f32[384,1536]{1,0:T(8,128)}) custom-call(bf16[1536,384]{1,0:T(8,128)(2,1)} %get-tuple-element.90.refs_0_, bf16[1536,384]{1,0:T(8,128)(2,1)} %get-tuple-element.86.refs_1_, bf16[1536,384]{1,0:T(8,128)(2,1)} %get-tuple-element.87.refs_2_, bf16[1536,384]{1,0:T(8,128)(2,1)} %refs_3_.1, bf16[1536,384]{1,0:T(8,128)(2,1)} %refs_4_.1, ...), custom_call_target="tpu_custom_call" | custom-call | flops 5435817984 | bytes 7077888 | tf_op jit(solution)/shard_map/scatter_both/pallas_call | solution.py:1089
  783.8 7.5 multiply_reduce_fusion.13
  791.7 5.0 fusion.14
  796.8 4.2 all-to-all-start.1
  801.7 2.2 copy.109
  804.0 23.3 %small_exchange_tp_7.1 = (f32[4,24,384]{2,1,0:T(8,128)}, bf16[4,384,192]{2,1,0:T(8,128)(2,1)}) custom-call(f32[4,24,384]{2,1,0:T(8,128)} %pad.21.refs_0_, bf16[4,384,192]{2,1,0:T(8,128)(2,1)} %bitcast.154), custom_call_target="tpu_custom_call" | custom-call | tf_op jit(solution)/shard_map/small_exchange_tp_7/pallas_call | solution.py:584
  830.9 12.8 %small_gather_seq_8.1 = (f32[8,24,384]{2,1,0:T(8,128)}, f32[8,16,128]{2,1,0:T(8,128)}, bf16[8,16,1024]{2,1,0:T(8,128)(2,1)}) custom-call(f32[24,384]{1,0:T(8,128)} %reduce_sum.349.refs_0_, f32[16,128]{1,0:T(8,128)} %pad.23.refs_1_, bf16[16,1024]{1,0:T(8,128)(2,1)} %pad.24.refs_2_), custom_call_target="tpu_custom_call" | custom-call | tf_op jit(solution)/shard_map/small_gather_seq_8/pallas_call | solution.py:408
  853.0 3.5 reshape.232
  862.6 2.2 fusion.28
  864.8 2.4 fusion.22
  (273 shorter events, 60.0 us)
Async XLA Ops:
  7.2 133.0 %copy-start = (bf16[1024,1536]{1,0:T(8,128)(2,1)S(1)}, bf16[1024,1536]{1,0:T(8,128)(2,1)}, u32[]{:S(2)}) copy-start(bf16[1024,1536]{1,0:T(8,128)(2,1)} %param.34) | copy-start | bytes 9437188
  7.2 6.8 copy-start.37
  7.2 192.6 %all-gather.7.cloned.1.call-start = ((), (), s32[]{:S(2)}) async-start(), calls=%async_computation.6 | async-start | bytes 3932160 | tf_op jit(solution)/shard_map/all_gather | solution.py:1251
  8.2 130.7 %copy-start.44 = (s32[3]{0:T(128)}, s32[3]{0:T(128)S(1)}, u32[]{:S(2)}) copy-start(s32[3]{0:T(128)S(1)} %select_reduce_fusion.5) | copy-start | bytes 40
  8.9 130.0 %copy-start.46 = (s32[3]{0:T(128)}, s32[3]{0:T(128)S(1)}, u32[]{:S(2)}) copy-start(s32[3]{0:T(128)S(1)} %fusion.42) | copy-start | bytes 40
  10.5 20.9 %copy-start.41 = (f32[384]{0:T(512)}, f32[384]{0:T(512)S(1)}, u32[]{:S(2)}) copy-start(f32[384]{0:T(512)S(1)} %add_rsqrt_fusion.1) | copy-start | bytes 4612
  10.6 20.8 %copy-start.19 = (f32[384]{0:T(512)}, f32[384]{0:T(512)S(1)}, u32[]{:S(2)}) copy-start(f32[384]{0:T(512)S(1)} %get-tuple-element.207) | copy-start | bytes 4612
  10.6 20.8 %copy-start.21 = (f32[384]{0:T(512)}, f32[384]{0:T(512)S(1)}, u32[]{:S(2)}) copy-start(f32[384]{0:T(512)S(1)} %get-tuple-element.208) | copy-start | bytes 4612
  10.6 20.8 %copy-start.23 = (f32[384]{0:T(512)}, f32[384]{0:T(512)S(1)}, u32[]{:S(2)}) copy-start(f32[384]{0:T(512)S(1)} %get-tuple-element.209) | copy-start | bytes 4612
  29.7 6.0 copy-start.27
  29.7 6.0 copy-start.29
  35.7 100.3 %copy-start.48 = (bf16[6,64]{1,0:T(8,128)(2,1)S(1)}, bf16[6,64]{1,0:T(8,128)(2,1)}, u32[]{:S(2)}) copy-start(bf16[6,64]{1,0:T(8,128)(2,1)} %param.39) | copy-start | bytes 2308
  35.8 101.0 %copy-start.49 = (bf16[6,64]{1,0:T(8,128)(2,1)S(1)}, bf16[6,64]{1,0:T(8,128)(2,1)}, u32[]{:S(2)}) copy-start(bf16[6,64]{1,0:T(8,128)(2,1)} %param.40) | copy-start | bytes 2308
  35.8 101.6 %copy-start.50 = (bf16[6,64]{1,0:T(8,128)(2,1)S(1)}, bf16[6,64]{1,0:T(8,128)(2,1)}, u32[]{:S(2)}) copy-start(bf16[6,64]{1,0:T(8,128)(2,1)} %param.41) | copy-start | bytes 2308
  35.8 102.3 %copy-start.64 = (bf16[6]{0:T(256)(128)(2,1)S(1)}, bf16[6]{0:T(256)(128)(2,1)}, u32[]{:S(2)}) copy-start(bf16[6]{0:T(256)(128)(2,1)} %param.42) | copy-start | bytes 40
  35.8 103.1 %copy-start.55 = (s32[1,3]{1,0:T(1,128)S(1)}, s32[1,3]{1,0:T(1,128)}, u32[]{:S(2)}) copy-start(s32[1,3]{1,0:T(1,128)} %param.26) | copy-start | bytes 40
  135.1 129.1 %all-gather.5.cloned.1.call-start = ((), (), s32[]{:S(2)}) async-start(), calls=%async_computation.5 | async-start | bytes 3932160 | tf_op jit(solution)/shard_map/all_gather | solution.py:1243
  135.9 242.9 %all-gather.9.cloned.1.call-start = ((), (), s32[]{:S(2)}) async-start(), calls=%async_computation.10 | async-start | bytes 5898240 | tf_op jit(solution)/shard_map/all_gather | solution.py:1258
  140.7 59.2 %copy-start.45 = (s32[3]{0:T(128)S(1)}, s32[3]{0:T(128)}, u32[]{:S(2)}) copy-start(s32[3]{0:T(128)} %copy-done.44) | copy-start | bytes 40
  140.7 59.3 %copy-start.47 = (s32[3]{0:T(128)S(1)}, s32[3]{0:T(128)}, u32[]{:S(2)}) copy-start(s32[3]{0:T(128)} %copy-done.46) | copy-start | bytes 40
  140.7 59.4 %copy-start.56 = (s32[1,3]{1,0:T(1,128)S(1)}, s32[1,3]{1,0:T(1,128)}, u32[]{:S(2)}) copy-start(s32[1,3]{1,0:T(1,128)} %param.27) | copy-start | bytes 40
  140.8 61.6 %copy-start.40 = (f32[1536]{0:T(1024)S(1)}, f32[1536]{0:T(1024)}, u32[]{:S(2)}) copy-start(f32[1536]{0:T(1024)} %convert_element_type.166) | copy-start | bytes 18436
  200.1 7.5 copy-start.43
  208.7 42.0 %copy-start.9 = (bf16[4096,384]{1,0:T(8,128)(2,1)S(1)}, bf16[4096,384]{1,0:T(8,128)(2,1)}, u32[]{:S(2)}) copy-start(bf16[4096,384]{1,0:T(8,128)(2,1)} %param.35) | copy-start | bytes 9437188
  289.3 56.3 %copy-start.2 = (bf16[384,1536]{1,0:T(8,128)(2,1)S(1)}, bf16[384,1536]{1,0:T(8,128)(2,1)}, u32[]{:S(2)}) copy-start(bf16[384,1536]{1,0:T(8,128)(2,1)} %param.22) | copy-start | bytes 3538948
  289.3 56.3 %copy-start.20 = (f32[384]{0:T(512)S(1)}, f32[384]{0:T(512)}, u32[]{:S(2)}) copy-start(f32[384]{0:T(512)} %copy-done.19) | copy-start | bytes 4612
  289.3 56.3 %copy-start.22 = (f32[384]{0:T(512)S(1)}, f32[384]{0:T(512)}, u32[]{:S(2)}) copy-start(f32[384]{0:T(512)} %copy-done.21) | copy-start | bytes 4612
  289.4 56.3 %copy-start.24 = (f32[384]{0:T(512)S(1)}, f32[384]{0:T(512)}, u32[]{:S(2)}) copy-start(f32[384]{0:T(512)} %copy-done.23) | copy-start | bytes 4612
  289.4 56.3 %copy-start.31 = (f32[1536]{0:T(1024)S(1)}, f32[1536]{0:T(1024)}, u32[]{:S(2)}) copy-start(f32[1536]{0:T(1024)} %get-tuple-element.191) | copy-start | bytes 18436
  289.4 56.3 %copy-start.32 = (f32[1536]{0:T(1024)S(1)}, f32[1536]{0:T(1024)}, u32[]{:S(2)}) copy-start(f32[1536]{0:T(1024)} %get-tuple-element.192) | copy-start | bytes 18436
  289.4 56.3 %copy-start.33 = (f32[1536]{0:T(1024)S(1)}, f32[1536]{0:T(1024)}, u32[]{:S(2)}) copy-start(f32[1536]{0:T(1024)} %get-tuple-element.193) | copy-start | bytes 18436
  522.9 33.1 %all-to-all-start = ((bf16[384,4,384]{2,0,1:T(8,128)(2,1)}), bf16[384,4,384]{2,0,1:T(8,128)(2,1)}, u32[]{:S(2)}, u32[]{:S(2)}) async-start(bf16[384,4,384]{2,0,1:T(8,128)(2,1)} %bitcast.150), calls=%async_computation | async-start | bytes 2359296 | tf_op jit(solution)/shard_map/all_to_all | solution.py:1297
  527.2 269.6 %reduce-scatter.8.cloned.1.call-start = ((), (), s32[]{:S(2)}) async-start(), calls=%async_computation.9 | async-start | bytes 5898240 | tf_op jit(solution)/shard_map/reduce_scatter | solution.py:1302
  556.1 245.7 %reduce-scatter.6.cloned.1.call-start = ((), (), s32[]{:S(2)}) async-start(), calls=%async_computation.8 | async-start | bytes 5308416 | tf_op jit(solution)/shard_map/reduce_scatter | solution.py:1296
  563.2 299.5 %reduce-scatter.4.cloned.1.call-start = ((), (), s32[]{:S(2)}) async-start(), calls=%async_computation.7 | async-start | bytes 11059200 | tf_op jit(solution)/shard_map/reduce_scatter | solution.py:1316
  643.4 14.0 %slice-start.2 = ((s8[4718592]{0:T(1024)(128)(4,1)}), s8[4194304]{0:T(1024)(128)(4,1)S(1)}, s32[]{:S(2)}) async-start(s8[4718592]{0:T(1024)(128)(4,1)} %bitcast.186), calls=%async_computation.13 | async-start | bytes 8388608
  650.6 6.8 slice-start.3
  676.5 107.2 %copy-start.3 = (bf16[384,1536]{1,0:T(8,128)(2,1)S(1)}, bf16[384,1536]{1,0:T(8,128)(2,1)}, u32[]{:S(2)}) copy-start(bf16[384,1536]{1,0:T(8,128)(2,1)} %param.22) | copy-start | bytes 3538948
  676.5 107.2 %copy-start.5 = (f32[384,1536]{1,0:T(8,128)S(1)}, f32[384,1536]{1,0:T(8,128)}, u32[]{:S(2)}) copy-start(f32[384,1536]{1,0:T(8,128)} %copy-done.4) | copy-start | bytes 7077892
  676.5 107.2 %copy-start.7 = (bf16[384,1536]{1,0:T(8,128)(2,1)S(1)}, bf16[384,1536]{1,0:T(8,128)(2,1)}, u32[]{:S(2)}) copy-start(bf16[384,1536]{1,0:T(8,128)(2,1)} %param.43) | copy-start | bytes 3538948
  676.5 107.2 %copy-start.14 = (f32[1536]{0:T(1024)S(1)}, f32[1536]{0:T(1024)}, u32[]{:S(2)}) copy-start(f32[1536]{0:T(1024)} %copy-done.13) | copy-start | bytes 18436
  676.5 107.2 %copy-start.16 = (f32[1536]{0:T(1024)S(1)}, f32[1536]{0:T(1024)}, u32[]{:S(2)}) copy-start(f32[1536]{0:T(1024)} %copy-done.15) | copy-start | bytes 18436
  676.5 107.2 %copy-start.18 = (f32[1536]{0:T(1024)S(1)}, f32[1536]{0:T(1024)}, u32[]{:S(2)}) copy-start(f32[1536]{0:T(1024)} %copy-done.17) | copy-start | bytes 18436
  676.5 107.2 %copy-start.26 = (f32[1536]{0:T(1024)S(1)}, f32[1536]{0:T(1024)}, u32[]{:S(2)}) copy-start(f32[1536]{0:T(1024)} %copy-done.25) | copy-start | bytes 18436
  676.5 107.2 %copy-start.28 = (f32[1536]{0:T(1024)S(1)}, f32[1536]{0:T(1024)}, u32[]{:S(2)}) copy-start(f32[1536]{0:T(1024)} %copy-done.27) | copy-start | bytes 18436
  676.6 107.2 %copy-start.30 = (f32[1536]{0:T(1024)S(1)}, f32[1536]{0:T(1024)}, u32[]{:S(2)}) copy-start(f32[1536]{0:T(1024)} %copy-done.29) | copy-start | bytes 18436
  676.6 107.2 %copy-start.42 = (f32[384]{0:T(512)S(1)}, f32[384]{0:T(512)}, u32[]{:S(2)}) copy-start(f32[384]{0:T(512)} %copy-done.41) | copy-start | bytes 4612
  796.8 54.7 %all-to-all-start.1 = ((bf16[1,384,8,192]{1,3,0,2:T(8,128)(2,1)}), bf16[1,384,8,192]{1,3,0,2:T(8,128)(2,1)S(1)}, u32[]{:S(2)}, u32[]{:S(2)}) async-start(bf16[1,384,8,192]{1,3,0,2:T(8,128)(2,1)} %bitcast.160), calls=%async_computation.4 | async-start | bytes 2359296 | tf_op jit(solution)/shard_map/all_to_all | solution.py:1303
  (30 other events, 89.9 us)
Sparse Core Ops, SparseCore 0:
  135.2 64.5 all-gather.6
  202.0 62.1 all-gather.4
  265.7 113.0 all-gather.8
  556.2 83.3 reduce-scatter.7
  642.9 54.3 reduce-scatter.5
  701.2 92.3 reduce-scatter.3
